TPU v7x, 512 devices: a whole 4x8x8 slice. The times are simulated.
512 devices in a mesh: row: 16 (over x, y_lo, core), blk: 32 (over z, y_hi).
Axes of the slice: x: 4, y: 8 (y_hi: 4, y_lo: 2; y = y_hi * 2 + y_lo), z: 8, core: 2. Of those that a mesh axis runs over, the one named last changes fastest.
Arguments:
- latent: float32 [28, 524288], P(None, ('row', 'blk')), may hold values from -3 to 3, as said below
- w_post: bfloat16 [28, 1024], replicated, may hold values from -1 to 1
- w_proj: bfloat16 [1024, 768], replicated, may hold values from -0.1875 to 0.1875
- gain: float32 [768], replicated, may hold values from 0.25 to 1.75
- text_embed: bfloat16 [1024, 768], P(('row', 'blk')), may hold values from -6 to 6
- labels: int32 [1024], P(('row', 'blk')), may hold values from 0 to 1023, each once
- logit_scale: float32 [1], replicated, may hold values from 20 to 40
- logit_bias: float32 [1], replicated, may hold values from -9 to -6
Outputs:
- grad_image: float32 [1024, 768], P(('row', 'blk'))
- grad_text: float32 [1024, 768], P(('row', 'blk'))
- scalars: float32 [3], replicated
Inputs may be any that keep to these rules, and one draw needn't show every extreme that they name: Every entry of latent has magnitude 0.3 or more. `labels`: each of the 1024 texts is the match of exactly one image.
All inputs are finite; a program needn't handle non-finite values.
Results may differ from a plain program's by a relative error of at most 0.0015.
The roundings to bfloat16 on the way count: a program that leaves them out, or rounds other values in their place, can miss the bound.
Values may be sent and summed in bfloat16 or wider, within the bound.
No kernel may reach another device: no remote copies, remote signals or barrier semaphores. Data moves between devices by JAX's collectives and lax.ppermute only.
A program may use at most 64 MiB of HBM per device.

v0:
```python
import functools
import math

import jax
import jax.numpy as jnp
from jax import lax
from jax.experimental import pallas as pl
from jax.experimental.pallas import tpu as pltpu
from jax.sharding import Mesh
from jax.sharding import PartitionSpec as P

EPS = 1e-06
SHARPNESS = 4.0
BITS = 28
SIDE = 128
CHUNK = 256

ROW_AXES = ("x", "y_lo", "core")
BLK_AXES = ("z", "y_hi")
TEXT_AXES = ("y_hi", "y_lo", "core")
IMAGE_AXES = ("x", "z")


def code_sums(latent):
    bit_count = latent.shape[0]
    length = jnp.sqrt(jnp.sum(latent * latent, axis=0, keepdims=True))
    unit_code = latent / length
    root = 1.0 / math.sqrt(bit_count)
    offset = unit_code - jnp.where(latent > 0, root, -root)
    sharp = SHARPNESS * math.sqrt(bit_count) * unit_code
    size = jnp.abs(sharp)
    small = jnp.exp(-size)
    inverse = 1.0 / (1.0 + small)
    rest = small * inverse
    entropy = jnp.log1p(small) + size * rest
    prob = jnp.where(sharp > 0, inverse, rest)

    def total(values):
        return jnp.sum(jnp.sum(values, axis=1, keepdims=True), axis=0, keepdims=True)

    usage = jnp.sum(prob, axis=1, keepdims=True)
    return (total(offset * offset), total(entropy), usage)


def round_bf(values):
    return values.astype(jnp.bfloat16).astype(jnp.float32)


def gelu(x):
    inner = x * (math.sqrt(2.0 / math.pi) + (math.sqrt(2.0 / math.pi) * 0.044715) * (x * x))
    half = 0.5 * x
    return half + half * jnp.tanh(inner)


def image_kernel(
    copies,
    latent_hbm,
    post_hbm,
    proj_hbm,
    gain_ref,
    label_ref,
    block_ref,
    unit_ref,
    inv_ref,
    latent_ref,
    post_ref,
    proj_ref,
    sems,
):
    fetch_latent = pltpu.make_async_copy(latent_hbm, latent_ref, sems.at[0])
    fetch_post = pltpu.make_async_copy(post_hbm, post_ref, sems.at[1])
    fetch_proj = pltpu.make_async_copy(proj_hbm, proj_ref, sems.at[2])
    fetch_latent.start()
    fetch_post.start()
    fetch_proj.start()
    fetch_latent.wait()
    latent = latent_ref[...]
    bit_count, token_count = latent.shape
    image_count, feat_width = unit_ref.shape
    patch = token_count // image_count

    commit, entropy, usage = code_sums(latent)
    lane = lax.broadcasted_iota(jnp.int32, (bit_count, SIDE), 1)
    bit = lax.broadcasted_iota(jnp.int32, (bit_count, SIDE), 0)
    first = round_bf(usage)
    second = round_bf(usage - first)
    third = usage - first - second
    spread = jnp.where(lane == bit, first, 0.0)
    spread = jnp.where(lane == bit + 32, second, spread)
    spread = jnp.where(lane == bit + 64, third, spread)
    side = jnp.sum(spread, axis=0, keepdims=True)
    place = lax.broadcasted_iota(jnp.int32, (1, SIDE), 1)
    for at, value in ((BITS, commit), (BITS + 1, entropy)):
        first = round_bf(value)
        second = round_bf(value - first)
        third = value - first - second
        side = jnp.where(place == at, first, side)
        side = jnp.where(place == at + 32, second, side)
        side = jnp.where(place == at + 64, third, side)
    sides = []
    for i in range(image_count):
        label = label_ref[i]
        high = (label // 32).astype(jnp.float32)
        low = (label % 32).astype(jnp.float32)
        own = side if i == 0 else jnp.zeros_like(side)
        own = jnp.where(place == SIDE - 2, high, own)
        sides.append(jnp.where(place == SIDE - 1, low, own))
    codes = jnp.where(latent > 0, 1.0, -1.0)
    codes = jnp.transpose(codes, (1, 0)).astype(jnp.bfloat16)
    fetch_post.wait()
    post = post_ref[...]
    fetch_proj.wait()
    proj = proj_ref[...]
    sums = []
    for first in range(0, token_count, CHUNK):
        pre_act = jnp.dot(codes[first : first + CHUNK], post, preferred_element_type=jnp.float32)
        hidden = gelu(pre_act).astype(jnp.bfloat16)
        projected = jnp.dot(hidden, proj, preferred_element_type=jnp.float32)
        square = jnp.sum(projected * projected, axis=-1, keepdims=True)
        scaled = projected * lax.rsqrt(square * (1.0 / feat_width) + EPS)
        sums.append(jnp.sum(scaled, axis=0, keepdims=True))
    steps = patch // CHUNK
    rows = [functools.reduce(jnp.add, sums[i * steps : (i + 1) * steps]) for i in range(image_count)]
    embeds = jnp.concatenate(rows, axis=0) * gain_ref[...][None, :] * (1.0 / patch)
    inverse = lax.rsqrt(jnp.sum(embeds * embeds, axis=-1, keepdims=True) + EPS)
    unit = embeds * inverse
    unit_ref[...] = unit
    inv_ref[...] = jnp.broadcast_to(inverse, inv_ref.shape)

    block = jnp.concatenate([unit, jnp.concatenate(sides, axis=0)], axis=1)
    block = block.astype(jnp.bfloat16)
    for member in range(copies):
        block_ref[member] = block


def embed_images(latent, w_post, w_proj, gain, labels, copies):
    image_count = labels.shape[0]
    feat_width = w_proj.shape[1]
    vmem = pl.BlockSpec(memory_space=pltpu.VMEM)
    hbm = pl.BlockSpec(memory_space=pl.ANY)
    return pl.pallas_call(
        functools.partial(image_kernel, copies),
        out_shape=(
            jax.ShapeDtypeStruct((copies, image_count, feat_width + SIDE), jnp.bfloat16),
            jax.ShapeDtypeStruct((image_count, feat_width), jnp.float32),
            jax.ShapeDtypeStruct((image_count, 128), jnp.float32),
        ),
        in_specs=[hbm, hbm, hbm, vmem, pl.BlockSpec(memory_space=pltpu.SMEM)],
        out_specs=(vmem, vmem, vmem),
        scratch_shapes=[
            pltpu.VMEM(latent.shape, latent.dtype),
            pltpu.VMEM(w_post.shape, w_post.dtype),
            pltpu.VMEM(w_proj.shape, w_proj.dtype),
            pltpu.SemaphoreType.DMA((3,)),
        ],
        compiler_params=pltpu.CompilerParams(vmem_limit_bytes=56 * 1024 * 1024),
        cost_estimate=pl.CostEstimate(
            flops=2_200_000_000, bytes_accessed=1_800_000, transcendentals=1_100_000
        ),
        name="embed_images",
    )(latent, w_post, w_proj, gain, labels)


def unit_rows(values):
    inverse = lax.rsqrt(jnp.sum(values * values, axis=-1, keepdims=True) + EPS)
    return (values * inverse, inverse)


def tangent(direction, unit, inverse):
    return (direction - unit * jnp.sum(unit * direction, axis=-1, keepdims=True)) * inverse


def text_kernel(text_ref, block_ref, unit_ref, inv_ref):
    unit, inverse = unit_rows(text_ref[...].astype(jnp.float32))
    block_ref[...] = jnp.broadcast_to(unit.astype(jnp.bfloat16)[None], block_ref.shape)
    unit_ref[...] = unit
    inv_ref[...] = jnp.broadcast_to(inverse, inv_ref.shape)


def text_blocks(text_embed, copies):
    rows = text_embed.shape[0]
    vmem = pl.BlockSpec(memory_space=pltpu.VMEM)
    return pl.pallas_call(
        text_kernel,
        out_shape=(
            jax.ShapeDtypeStruct((copies,) + text_embed.shape, jnp.bfloat16),
            jax.ShapeDtypeStruct(text_embed.shape, jnp.float32),
            jax.ShapeDtypeStruct((rows, 128), jnp.float32),
        ),
        in_specs=[vmem],
        out_specs=(vmem, vmem, vmem),
        name="text_blocks",
    )(text_embed)


def finish_kernel(total_tokens, parts_ref, unit_ref, inv_ref, scale_ref, grad_ref, scalar_ref):
    feat_width = unit_ref.shape[-1]
    total = parts_ref[0]
    for member in range(1, parts_ref.shape[0]):
        total = total + parts_ref[member]
    direction = scale_ref[0] * total[:, :feat_width]
    grad_ref[...] = tangent(direction, unit_ref[...], inv_ref[...][:, :1])
    side = total[:1, feat_width:]
    means = side[:, :32] + side[:, 32:64] + side[:, 64:96]
    means = means * (1.0 / total_tokens)
    place = lax.broadcasted_iota(jnp.int32, means.shape, 1)
    usage = jnp.where(place < BITS, means, 0.5)
    spread = -(usage * jnp.log(usage) + (1.0 - usage) * jnp.log(1.0 - usage))
    scalar_ref[0] = jnp.sum(jnp.where(place == BITS, means, 0.0))
    scalar_ref[1] = jnp.sum(jnp.where(place == BITS + 1, means, 0.0))
    scalar_ref[2] = jnp.sum(jnp.where(place < BITS, spread, 0.0))


def finish_text(parts, text_unit, text_inv, logit_scale, total_tokens):
    vmem = pl.BlockSpec(memory_space=pltpu.VMEM)
    smem = pl.BlockSpec(memory_space=pltpu.SMEM)
    return pl.pallas_call(
        functools.partial(finish_kernel, total_tokens),
        out_shape=(
            jax.ShapeDtypeStruct(text_unit.shape, jnp.float32),
            jax.ShapeDtypeStruct((3,), jnp.float32),
        ),
        in_specs=[vmem, vmem, vmem, smem],
        out_specs=(vmem, smem),
        name="finish_text",
    )(parts, text_unit, text_inv, logit_scale)


def group_ids(sizes, axes, pair_count):
    count = math.prod(sizes[axis] for axis in axes)
    member = jnp.arange(count * pair_count, dtype=jnp.int32) // pair_count
    place = {axis: lax.axis_index(axis) for axis in ROW_AXES + BLK_AXES}
    for axis in reversed(axes):
        place[axis] = member % sizes[axis]
        member = member // sizes[axis]
    device = jnp.int32(0)
    for axis in ROW_AXES + BLK_AXES:
        device = device * sizes[axis] + place[axis]
    return device * pair_count + jnp.arange(count * pair_count, dtype=jnp.int32) % pair_count


def body(sizes, latent, w_post, w_proj, gain, text_embed, labels, logit_scale, logit_bias):
    pair_count, feat_width = text_embed.shape
    n_image = math.prod(sizes[axis] for axis in IMAGE_AXES)
    n_text = math.prod(sizes[axis] for axis in TEXT_AXES)
    text_count = n_text * pair_count
    total_tokens = latent.shape[1] * math.prod(sizes.values())
    scale_value = logit_scale[0]
    bias_value = logit_bias[0]

    text_block, text_unit, text_inv = text_blocks(text_embed, n_text)
    group_text = lax.all_to_all(text_block, TEXT_AXES, 0, 0)

    image_block, image_unit, image_inv = embed_images(
        latent, w_post, w_proj, gain, labels, n_image
    )
    image_block, group_text = lax.optimization_barrier((image_block, group_text))
    group_text = group_text.reshape(text_count, feat_width)
    group_block = lax.all_to_all(image_block, IMAGE_AXES, 0, 0)
    group_block = group_block.reshape(n_image * pair_count, feat_width + SIDE)
    group_image = group_block[:, :feat_width]
    group_side = group_block[:, feat_width:].astype(jnp.float32)
    group_labels = (group_side[:, SIDE - 2] * 32.0 + group_side[:, SIDE - 1]).astype(jnp.int32)
    group_sums = jnp.sum(group_side, axis=0, keepdims=True)

    text_ids = group_ids(sizes, TEXT_AXES, pair_count)
    products = jnp.dot(group_image, group_text.T, preferred_element_type=jnp.float32)
    pair_sign = jnp.where(
        group_labels[:, None] == text_ids[None, :], jnp.float32(1.0), jnp.float32(-1.0)
    )
    margin = pair_sign * (scale_value * products + bias_value)
    grad_bf = (-pair_sign * jax.nn.sigmoid(-margin)).astype(jnp.bfloat16)
    text_part = jnp.dot(grad_bf.T, group_image, preferred_element_type=jnp.float32)
    text_part = jnp.concatenate(
        [text_part, jnp.broadcast_to(group_sums, (text_count, SIDE))], axis=1
    )
    text_part = text_part.reshape(n_text, pair_count, feat_width + SIDE)
    text_part = lax.all_to_all(text_part, TEXT_AXES, 0, 0)

    image_part = jnp.dot(grad_bf, group_text, preferred_element_type=jnp.float32)
    image_part = image_part.reshape(n_image, pair_count, feat_width)
    image_part, text_part = lax.optimization_barrier((image_part, text_part))
    image_part = lax.all_to_all(image_part, IMAGE_AXES, 0, 0)
    image_dir = scale_value * jnp.sum(image_part, axis=0)
    grad_image = tangent(image_dir, image_unit, image_inv[:, :1])
    grad_text, scalars = finish_text(text_part, text_unit, text_inv, logit_scale, total_tokens)
    return (grad_image, grad_text, scalars)


def solution(mesh):
    sizes = {"x": 4, "y_lo": 2, "core": 2, "z": 8, "y_hi": 4}
    names = ROW_AXES + BLK_AXES
    fine = Mesh(mesh.devices.reshape([sizes[axis] for axis in names]), names)
    return jax.shard_map(
        functools.partial(body, sizes),
        mesh=fine,
        in_specs=(P(None, names), P(), P(), P(), P(names, None), P(names), P(), P()),
        out_specs=(P(names, None), P(names, None), P()),
        check_vma=False,
    )
```

profile of v0, /device:TPU:1, one launch (start us, length us, event | category | flops | bytes accessed | tf_op | source)
XLA Modules:
  0.0 73.4 jit_solution(9761713161544782701)
XLA Ops:
  0.6 1.4 %text_blocks.1 = (bf16[16,2,768]{2,1,0:T(2,128)(2,1)}, f32[2,768]{1,0:T(2,128)}, f32[2,128]{1,0:T(2,128)}) custom-call(bf16[2,768]{1,0:T(2,128)(2,1)} %text_ref.1), custom_call_target="tpu_custom_call" | custom-call | tf_op jit(solution)/shard_map/text_blocks/pallas_call | solution.py:183
  2.0 10.1 %all-to-all-start = ((bf16[16,2,768]{2,1,0:T(2,128)(2,1)}), bf16[16,2,768]{2,1,0:T(2,128)(2,1)S(1)}, u32[]{:S(2)}, u32[]{:S(2)}) async-start(bf16[16,2,768]{2,1,0:T(2,128)(2,1)} %get-tuple-element.16), calls=%async_computation | async-start | bytes 98304 | tf_op jit(solution)/shard_map/all_to_all | solution.py:252
  12.2 5.9 %embed_images.1 = (bf16[32,2,896]{2,1,0:T(2,128)(2,1)}, f32[2,768]{1,0:T(2,128)}, f32[2,128]{1,0:T(2,128)}) custom-call(f32[28,1024]{1,0:T(8,128)} %latent_hbm.1, bf16[28,1024]{1,0:T(8,128)(2,1)} %post_hbm.1, bf16[1024,768]{1,0:T(8,128)(2,1)} %proj_hbm.1, f32[768]{0:T(1024)} %gain_ref.1, s32[2]{0:T(128)} %label_ref.1), custom_call_target="tpu_custom_call" | custom-call | flops 2200000000 | bytes 1800000 | tf_op jit(solution)/shard_map/embed_images/pallas_call | solution.py:141
  18.1 0.0 copy-start.2
  18.1 1.6 %all-to-all-done = bf16[16,2,768]{2,1,0:T(2,128)(2,1)S(1)} async-done(((bf16[16,2,768]{2,1,0:T(2,128)(2,1)}), bf16[16,2,768]{2,1,0:T(2,128)(2,1)S(1)}, u32[]{:S(2)}, u32[]{:S(2)}) %all-to-all-start) | async-done | bytes 49184 | tf_op jit(solution)/shard_map/all_to_all | solution.py:252
  19.7 11.3 %all-to-all-start.1 = ((bf16[32,2,896]{2,1,0:T(2,128)(2,1)}), bf16[32,2,896]{2,1,0:T(2,128)(2,1)S(1)}, u32[]{:S(2)}, u32[]{:S(2)}) async-start(bf16[32,2,896]{2,1,0:T(2,128)(2,1)} %get-tuple-element.17), calls=%async_computation.1 | async-start | bytes 229376 | tf_op jit(solution)/shard_map/all_to_all | solution.py:259
  32.4 0.0 copy-start.1
  32.4 7.7 %all-to-all-done.1 = bf16[32,2,896]{2,1,0:T(2,128)(2,1)S(1)} async-done(((bf16[32,2,896]{2,1,0:T(2,128)(2,1)}), bf16[32,2,896]{2,1,0:T(2,128)(2,1)S(1)}, u32[]{:S(2)}, u32[]{:S(2)}) %all-to-all-start.1) | async-done | bytes 114720 | tf_op jit(solution)/shard_map/all_to_all | solution.py:259
  40.2 0.1 copy.20
  40.3 0.1 convert_reduce_fusion
  40.5 0.2 fusion.6
  40.6 0.1 fusion.7
  40.8 0.1 copy.17
  40.9 0.7 reshape.115
  41.6 7.2 %all-to-all-start.2 = ((f32[16,2,896]{2,1,0:T(2,128)}), f32[16,2,896]{2,1,0:T(2,128)S(1)}, u32[]{:S(2)}, u32[]{:S(2)}) async-start(f32[16,2,896]{2,1,0:T(2,128)} %reshape.115), calls=%async_computation.2 | async-start | bytes 229376 | tf_op jit(solution)/shard_map/all_to_all | solution.py:278
  48.8 0.1 fusion.10
  48.9 8.7 %all-to-all-done.2.parts_ref = f32[16,2,896]{2,1,0:T(2,128)S(1)} async-done(((f32[16,2,896]{2,1,0:T(2,128)}), f32[16,2,896]{2,1,0:T(2,128)S(1)}, u32[]{:S(2)}, u32[]{:S(2)}) %all-to-all-start.2) | async-done | bytes 114720 | tf_op jit(solution)/shard_map/all_to_all | solution.py:278
  57.6 0.0 copy-start
  57.6 0.8 %copy.19 = f32[32,2,768]{2,1,0:T(2,128)} copy(f32[32,2,768]{2,0,1:T(8,128)S(1)} %fusion.10) | data formatting | bytes 393216 | tf_op jit(solution)/shard_map/optimization_barrier | solution.py:282
  58.4 3.9 %all-to-all-start.3 = ((f32[32,2,768]{2,1,0:T(2,128)}), f32[32,2,768]{2,1,0:T(2,128)S(1)}, u32[]{:S(2)}, u32[]{:S(2)}) async-start(f32[32,2,768]{2,1,0:T(2,128)} %copy.19), calls=%async_computation.3 | async-start | bytes 393216 | tf_op jit(solution)/shard_map/all_to_all | solution.py:283
  62.3 0.0 copy-done.2
  62.3 0.1 slice_reduce_fusion
  62.4 0.0 copy-done
  62.4 1.7 %finish_text.1 = (f32[2,768]{1,0:T(2,128)}, f32[3]{0:T(128)}) custom-call(f32[16,2,896]{2,1,0:T(2,128)} %copy-done, f32[2,768]{1,0:T(2,128)} %get-tuple-element.23.unit_ref, f32[2,128]{1,0:T(2,128)} %get-tuple-element.24.inv_ref, f32[1]{0:T(128)} %copy.23.scale_ref), custom_call_target="tpu_custom_call" | custom-call | tf_op jit(solution)/shard_map/finish_text/pallas_call | solution.py:217
  64.1 8.3 %all-to-all-done.3 = f32[32,2,768]{2,1,0:T(2,128)S(1)} async-done(((f32[32,2,768]{2,1,0:T(2,128)}), f32[32,2,768]{2,1,0:T(2,128)S(1)}, u32[]{:S(2)}, u32[]{:S(2)}) %all-to-all-start.3) | async-done | bytes 196640 | tf_op jit(solution)/shard_map/all_to_all | solution.py:283
  72.5 0.1 reduce_sum.28
  72.6 0.0 copy-done.1
  72.6 0.1 multiply_reduce_fusion
  72.7 0.7 subtract_multiply_fusion
  (9 shorter events, 0.2 us)
Async XLA Ops:
  2.0 17.6 %all-to-all-start = ((bf16[16,2,768]{2,1,0:T(2,128)(2,1)}), bf16[16,2,768]{2,1,0:T(2,128)(2,1)S(1)}, u32[]{:S(2)}, u32[]{:S(2)}) async-start(bf16[16,2,768]{2,1,0:T(2,128)(2,1)} %get-tuple-element.16), calls=%async_computation | async-start | bytes 98304 | tf_op jit(solution)/shard_map/all_to_all | solution.py:252
  18.1 44.2 %copy-start.2 = (f32[2,128]{1,0:T(2,128)S(1)}, f32[2,128]{1,0:T(2,128)}, u32[]{:S(2)}) copy-start(f32[2,128]{1,0:T(2,128)} %get-tuple-element.21) | copy-start | bytes 3076
  19.7 20.4 %all-to-all-start.1 = ((bf16[32,2,896]{2,1,0:T(2,128)(2,1)}), bf16[32,2,896]{2,1,0:T(2,128)(2,1)S(1)}, u32[]{:S(2)}, u32[]{:S(2)}) async-start(bf16[32,2,896]{2,1,0:T(2,128)(2,1)} %get-tuple-element.17), calls=%async_computation.1 | async-start | bytes 229376 | tf_op jit(solution)/shard_map/all_to_all | solution.py:259
  32.4 40.2 %copy-start.1 = (f32[2,768]{1,0:T(2,128)S(1)}, f32[2,768]{1,0:T(2,128)}, u32[]{:S(2)}) copy-start(f32[2,768]{1,0:T(2,128)} %get-tuple-element.20) | copy-start | bytes 18436
  41.6 16.0 %all-to-all-start.2 = ((f32[16,2,896]{2,1,0:T(2,128)}), f32[16,2,896]{2,1,0:T(2,128)S(1)}, u32[]{:S(2)}, u32[]{:S(2)}) async-start(f32[16,2,896]{2,1,0:T(2,128)} %reshape.115), calls=%async_computation.2 | async-start | bytes 229376 | tf_op jit(solution)/shard_map/all_to_all | solution.py:278
  57.6 4.8 %copy-start = (f32[16,2,896]{2,1,0:T(2,128)}, f32[16,2,896]{2,1,0:T(2,128)S(1)}, u32[]{:S(2)}) copy-start(f32[16,2,896]{2,1,0:T(2,128)S(1)} %all-to-all-done.2.parts_ref) | copy-start | bytes 344068
  58.4 14.0 %all-to-all-start.3 = ((f32[32,2,768]{2,1,0:T(2,128)}), f32[32,2,768]{2,1,0:T(2,128)S(1)}, u32[]{:S(2)}, u32[]{:S(2)}) async-start(f32[32,2,768]{2,1,0:T(2,128)} %copy.19), calls=%async_computation.3 | async-start | bytes 393216 | tf_op jit(solution)/shard_map/all_to_all | solution.py:283
where the time goes:
time: 73.9 us; the launch traced here: 73.4 us
  starting transfers between devices  32.5 us (44%)
  waiting for transfers between devices  26.3 us (36%)
  Pallas kernels  9.03 us (12%)
  between operations  2.07 us (3%)
  local copies, waits for them, and re-layouts  1.96 us (3%)
  other arithmetic  1.04 us (1%)
    all_to_all x1, starting transfers between devices, body(): group_block = lax.all_to_all(image_block, IMAGE_AXES, 0, 0)  11.3 us
    all_to_all x1, starting transfers between devices, body(): group_text = lax.all_to_all(text_block, TEXT_AXES, 0, 0)  10.1 us
    all_to_all x1, waiting for transfers between devices, body(): text_part = lax.all_to_all(text_part, TEXT_AXES, 0, 0)  8.69 us
    all_to_all x1, waiting for transfers between devices, body(): image_part = lax.all_to_all(image_part, IMAGE_AXES, 0, 0)  8.34 us
    all_to_all x1, waiting for transfers between devices, body(): group_block = lax.all_to_all(image_block, IMAGE_AXES, 0, 0)  7.7 us
    all_to_all x1, starting transfers between devices, body(): text_part = lax.all_to_all(text_part, TEXT_AXES, 0, 0)  7.19 us
    pallas_call x1, Pallas kernels, embed_images(): pl.pallas_call(functools.partial(image_kernel, copies), out_shape=(jax.Sh...  5.92 us
    all_to_all x1, starting transfers between devices, body(): image_part = lax.all_to_all(image_part, IMAGE_AXES, 0, 0)  3.87 us
  transfers between devices with their start and end apart: 4, of which 4 were waited for; matrix products, arithmetic and copies ran while one was open for 0% of the time, Pallas kernels for 10%

commit v1 on v0

--- a/solution.py
+++ b/solution.py
@@ -170,36 +170,61 @@
     return (direction - unit * jnp.sum(unit * direction, axis=-1, keepdims=True)) * inverse
 
 
-def text_kernel(text_ref, block_ref, unit_ref, inv_ref):
-    unit, inverse = unit_rows(text_ref[...].astype(jnp.float32))
-    block_ref[...] = jnp.broadcast_to(unit.astype(jnp.bfloat16)[None], block_ref.shape)
-    unit_ref[...] = unit
-    inv_ref[...] = jnp.broadcast_to(inverse, inv_ref.shape)
-
-
-def text_blocks(text_embed, copies):
-    rows = text_embed.shape[0]
+def tile_kernel(block_ref, text_ref, id_ref, scale_ref, bias_ref, text_part_ref, image_part_ref):
+    text_members, pair_count, feat_width = text_ref.shape
+    image_members = block_ref.shape[0]
+    block = [block_ref[member].astype(jnp.float32) for member in range(image_members)]
+    block = jnp.concatenate(block, axis=0)
+    image = block[:, :feat_width].astype(jnp.bfloat16)
+    side = block[:, feat_width:]
+    sums = jnp.broadcast_to(jnp.sum(side, axis=0, keepdims=True), (pair_count, SIDE))
+    label = side[:, SIDE - 2 : SIDE - 1] * 32.0 + side[:, SIDE - 1 : SIDE]
+    text = [text_ref[member].astype(jnp.float32) for member in range(text_members)]
+    text, _ = unit_rows(jnp.concatenate(text, axis=0))
+    text = text.astype(jnp.bfloat16)
+
+    products = lax.dot_general(
+        image, text, (((1,), (1,)), ((), ())), preferred_element_type=jnp.float32
+    )
+    pair_sign = jnp.where(label == id_ref[...].astype(jnp.float32), 1.0, -1.0)
+    margin = pair_sign * (scale_ref[0] * products + bias_ref[0])
+    grad = -pair_sign * jax.nn.sigmoid(-margin)
+    text_part = jnp.dot(
+        jnp.transpose(grad, (1, 0)).astype(jnp.bfloat16), image, preferred_element_type=jnp.float32
+    )
+    for member in range(text_members):
+        rows = text_part[member * pair_count : (member + 1) * pair_count]
+        text_part_ref[member] = jnp.concatenate([rows, sums], axis=1)
+    image_part = jnp.dot(grad.astype(jnp.bfloat16), text, preferred_element_type=jnp.float32)
+    for member in range(image_members):
+        image_part_ref[member] = image_part[member * pair_count : (member + 1) * pair_count]
+
+
+def score_tile(group_block, group_text, text_ids, logit_scale, logit_bias):
+    image_members, pair_count, _ = group_block.shape
+    text_members, _, feat_width = group_text.shape
     vmem = pl.BlockSpec(memory_space=pltpu.VMEM)
+    smem = pl.BlockSpec(memory_space=pltpu.SMEM)
     return pl.pallas_call(
-        text_kernel,
+        tile_kernel,
         out_shape=(
-            jax.ShapeDtypeStruct((copies,) + text_embed.shape, jnp.bfloat16),
-            jax.ShapeDtypeStruct(text_embed.shape, jnp.float32),
-            jax.ShapeDtypeStruct((rows, 128), jnp.float32),
+            jax.ShapeDtypeStruct((text_members, pair_count, feat_width + SIDE), jnp.float32),
+            jax.ShapeDtypeStruct((image_members, pair_count, feat_width), jnp.float32),
         ),
-        in_specs=[vmem],
-        out_specs=(vmem, vmem, vmem),
-        name="text_blocks",
-    )(text_embed)
-
-
-def finish_kernel(total_tokens, parts_ref, unit_ref, inv_ref, scale_ref, grad_ref, scalar_ref):
-    feat_width = unit_ref.shape[-1]
+        in_specs=[vmem, vmem, vmem, smem, smem],
+        out_specs=(vmem, vmem),
+        name="score_tile",
+    )(group_block, group_text, text_ids.reshape(1, -1), logit_scale, logit_bias)
+
+
+def finish_kernel(total_tokens, parts_ref, text_ref, scale_ref, grad_ref, scalar_ref):
+    feat_width = text_ref.shape[-1]
     total = parts_ref[0]
     for member in range(1, parts_ref.shape[0]):
         total = total + parts_ref[member]
     direction = scale_ref[0] * total[:, :feat_width]
-    grad_ref[...] = tangent(direction, unit_ref[...], inv_ref[...][:, :1])
+    unit, inverse = unit_rows(text_ref[...].astype(jnp.float32))
+    grad_ref[...] = tangent(direction, unit, inverse)
     side = total[:1, feat_width:]
     means = side[:, :32] + side[:, 32:64] + side[:, 64:96]
     means = means * (1.0 / total_tokens)
@@ -211,19 +236,19 @@
     scalar_ref[2] = jnp.sum(jnp.where(place < BITS, spread, 0.0))
 
 
-def finish_text(parts, text_unit, text_inv, logit_scale, total_tokens):
+def finish_text(parts, text_embed, logit_scale, total_tokens):
     vmem = pl.BlockSpec(memory_space=pltpu.VMEM)
     smem = pl.BlockSpec(memory_space=pltpu.SMEM)
     return pl.pallas_call(
         functools.partial(finish_kernel, total_tokens),
         out_shape=(
-            jax.ShapeDtypeStruct(text_unit.shape, jnp.float32),
+            jax.ShapeDtypeStruct(text_embed.shape, jnp.float32),
             jax.ShapeDtypeStruct((3,), jnp.float32),
         ),
-        in_specs=[vmem, vmem, vmem, smem],
+        in_specs=[vmem, vmem, smem],
         out_specs=(vmem, smem),
         name="finish_text",
-    )(parts, text_unit, text_inv, logit_scale)
+    )(parts, text_embed, logit_scale)
 
 
 def group_ids(sizes, axes, pair_count):
@@ -240,50 +265,29 @@
 
 
 def body(sizes, latent, w_post, w_proj, gain, text_embed, labels, logit_scale, logit_bias):
-    pair_count, feat_width = text_embed.shape
+    pair_count = text_embed.shape[0]
     n_image = math.prod(sizes[axis] for axis in IMAGE_AXES)
     n_text = math.prod(sizes[axis] for axis in TEXT_AXES)
-    text_count = n_text * pair_count
     total_tokens = latent.shape[1] * math.prod(sizes.values())
-    scale_value = logit_scale[0]
-    bias_value = logit_bias[0]
-
-    text_block, text_unit, text_inv = text_blocks(text_embed, n_text)
-    group_text = lax.all_to_all(text_block, TEXT_AXES, 0, 0)
+
+    text_copies = jnp.broadcast_to(text_embed[None], (n_text,) + text_embed.shape)
+    group_text = lax.all_to_all(text_copies, TEXT_AXES, 0, 0)
 
     image_block, image_unit, image_inv = embed_images(
         latent, w_post, w_proj, gain, labels, n_image
     )
     image_block, group_text = lax.optimization_barrier((image_block, group_text))
-    group_text = group_text.reshape(text_count, feat_width)
     group_block = lax.all_to_all(image_block, IMAGE_AXES, 0, 0)
-    group_block = group_block.reshape(n_image * pair_count, feat_width + SIDE)
-    group_image = group_block[:, :feat_width]
-    group_side = group_block[:, feat_width:].astype(jnp.float32)
-    group_labels = (group_side[:, SIDE - 2] * 32.0 + group_side[:, SIDE - 1]).astype(jnp.int32)
-    group_sums = jnp.sum(group_side, axis=0, keepdims=True)
-
     text_ids = group_ids(sizes, TEXT_AXES, pair_count)
-    products = jnp.dot(group_image, group_text.T, preferred_element_type=jnp.float32)
-    pair_sign = jnp.where(
-        group_labels[:, None] == text_ids[None, :], jnp.float32(1.0), jnp.float32(-1.0)
-    )
-    margin = pair_sign * (scale_value * products + bias_value)
-    grad_bf = (-pair_sign * jax.nn.sigmoid(-margin)).astype(jnp.bfloat16)
-    text_part = jnp.dot(grad_bf.T, group_image, preferred_element_type=jnp.float32)
-    text_part = jnp.concatenate(
-        [text_part, jnp.broadcast_to(group_sums, (text_count, SIDE))], axis=1
-    )
-    text_part = text_part.reshape(n_text, pair_count, feat_width + SIDE)
+    text_part, image_part = score_tile(
+        group_block, group_text, text_ids, logit_scale, logit_bias
+    )
     text_part = lax.all_to_all(text_part, TEXT_AXES, 0, 0)
-
-    image_part = jnp.dot(grad_bf, group_text, preferred_element_type=jnp.float32)
-    image_part = image_part.reshape(n_image, pair_count, feat_width)
     image_part, text_part = lax.optimization_barrier((image_part, text_part))
     image_part = lax.all_to_all(image_part, IMAGE_AXES, 0, 0)
-    image_dir = scale_value * jnp.sum(image_part, axis=0)
+    image_dir = logit_scale[0] * jnp.sum(image_part, axis=0)
     grad_image = tangent(image_dir, image_unit, image_inv[:, :1])
-    grad_text, scalars = finish_text(text_part, text_unit, text_inv, logit_scale, total_tokens)
+    grad_text, scalars = finish_text(text_part, text_embed, logit_scale, total_tokens)
     return (grad_image, grad_text, scalars)
 
 

time: 73.9 us -> 75.9 us (1.027)
  blocking collectives: 0 us -> 16.1 us
  waiting for transfers between devices: 26.3 us -> 16.5 us
  starting transfers between devices: 32.5 us -> 25.3 us
  other arithmetic: 1.04 us -> 2.79 us
  local copies, waits for them, and re-layouts: 1.96 us -> 2.77 us
    all_to_all x0 -> x1, blocking collectives: none -> 16.1 us  [body(): text_part = lax.all_to_all(text_part, TEXT_AXES, 0, 0)]
    all_to_all x2 -> x1, waiting for transfers between devices: 10.3 us -> 1.59 us  [body(): group_text = lax.all_to_all(text_copies, TEXT_AXES, 0, 0)]
    all_to_all x2 -> x1, starting transfers between devices: 17.3 us -> 10.1 us  [body(): group_text = lax.all_to_all(text_copies, TEXT_AXES, 0, 0)]
    broadcast_in_dim x0 -> x1, local copies, waits for them, and re-layouts: none -> 1.33 us  [body(): jnp.broadcast_to(text_embed[None], (n_text,) + text_embed.shape)]
    optimization_barrier x1 -> x0, local copies, waits for them, and re-layouts: 0.82 us -> none  [body(): image_part, text_part = lax.optimization_barrier((image_part, text_part))]
    reshape x4 -> x0, local copies, waits for them, and re-layouts: 0.79 us -> none  [the longest x1 0.7 us: body(): text_part = text_part.reshape(n_text, pair_count, feat_width + SIDE)]
  transfers between devices with their start and end apart: 4 -> 3, of which waited for: 4 -> 3; matrix products, arithmetic and copies ran while one was open for 0% -> 2% of each run, Pallas kernels for 10% -> 10%
where the time goes in v1:
time: 75.9 us; the launch traced here: 75.2 us
  starting transfers between devices  25.3 us (33%)
  waiting for transfers between devices  16.5 us (22%)
  blocking collectives  16.1 us (21%)
  Pallas kernels  9.75 us (13%)
  other arithmetic  2.79 us (4%)
  local copies, waits for them, and re-layouts  2.77 us (4%)
  between operations  1.97 us (3%)
    all_to_all x1, blocking collectives, body(): text_part = lax.all_to_all(text_part, TEXT_AXES, 0, 0)  16.1 us
    all_to_all x1, starting transfers between devices, body(): group_block = lax.all_to_all(image_block, IMAGE_AXES, 0, 0)  11.3 us
    all_to_all x1, starting transfers between devices, body(): group_text = lax.all_to_all(text_copies, TEXT_AXES, 0, 0)  10.1 us
    all_to_all x1, waiting for transfers between devices, body(): image_part = lax.all_to_all(image_part, IMAGE_AXES, 0, 0)  7.68 us
    all_to_all x1, waiting for transfers between devices, body(): group_block = lax.all_to_all(image_block, IMAGE_AXES, 0, 0)  7.25 us
    pallas_call x1, Pallas kernels, embed_images(): pl.pallas_call(functools.partial(image_kernel, copies), out_shape=(jax.Sh...  5.92 us
    all_to_all x1, starting transfers between devices, body(): image_part = lax.all_to_all(image_part, IMAGE_AXES, 0, 0)  3.86 us
    pallas_call x1, Pallas kernels, score_tile(): pl.pallas_call(tile_kernel, out_shape=(jax.ShapeDtypeStruct((text_members...  2.14 us
  transfers between devices with their start and end apart: 3, of which 3 were waited for; matrix products, arithmetic and copies ran while one was open for 2% of the time, Pallas kernels for 10%

profile of v1, /device:TPU:1, one launch (start us, length us, event | category | flops | bytes accessed | tf_op | source)
XLA Modules:
  0.0 75.2 jit_solution(1674068953534402145)
XLA Ops:
  0.6 1.3 %broadcast_in_dim.2 = bf16[16,2,768]{2,1,0:T(2,128)(2,1)} broadcast(bf16[2,768]{1,0:T(2,128)(2,1)} %text_ref.1), dimensions={1,2} | broadcast | bytes 52224 | tf_op jit(solution)/shard_map/broadcast_in_dim | solution.py:273
  2.0 10.1 %all-to-all-start = ((bf16[16,2,768]{2,1,0:T(2,128)(2,1)}), bf16[16,2,768]{2,1,0:T(2,128)(2,1)S(1)}, u32[]{:S(2)}, u32[]{:S(2)}) async-start(bf16[16,2,768]{2,1,0:T(2,128)(2,1)} %broadcast_in_dim.2), calls=%async_computation | async-start | bytes 98304 | tf_op jit(solution)/shard_map/all_to_all | solution.py:274
  12.1 5.9 %embed_images.1 = (bf16[32,2,896]{2,1,0:T(2,128)(2,1)}, f32[2,768]{1,0:T(2,128)}, f32[2,128]{1,0:T(2,128)}) custom-call(f32[28,1024]{1,0:T(8,128)} %latent_hbm.1, bf16[28,1024]{1,0:T(8,128)(2,1)} %post_hbm.1, bf16[1024,768]{1,0:T(8,128)(2,1)} %proj_hbm.1, f32[768]{0:T(1024)} %gain_ref.1, s32[2]{0:T(128)} %label_ref.1), custom_call_target="tpu_custom_call" | custom-call | flops 2200000000 | bytes 1800000 | tf_op jit(solution)/shard_map/embed_images/pallas_call | solution.py:141
  18.0 1.6 %all-to-all-done.text_ref = bf16[16,2,768]{2,1,0:T(2,128)(2,1)S(1)} async-done(((bf16[16,2,768]{2,1,0:T(2,128)(2,1)}), bf16[16,2,768]{2,1,0:T(2,128)(2,1)S(1)}, u32[]{:S(2)}, u32[]{:S(2)}) %all-to-all-start) | async-done | bytes 49184 | tf_op jit(solution)/shard_map/all_to_all | solution.py:274
  19.6 0.0 copy-start.1
  19.6 11.3 %all-to-all-start.1 = ((bf16[32,2,896]{2,1,0:T(2,128)(2,1)}), bf16[32,2,896]{2,1,0:T(2,128)(2,1)S(1)}, u32[]{:S(2)}, u32[]{:S(2)}) async-start(bf16[32,2,896]{2,1,0:T(2,128)(2,1)} %get-tuple-element.15), calls=%async_computation.1 | async-start | bytes 229376 | tf_op jit(solution)/shard_map/all_to_all | solution.py:280
  32.3 0.5 fusion.id_ref
  32.8 7.3 %all-to-all-done.1.block_ref = bf16[32,2,896]{2,1,0:T(2,128)(2,1)S(1)} async-done(((bf16[32,2,896]{2,1,0:T(2,128)(2,1)}), bf16[32,2,896]{2,1,0:T(2,128)(2,1)S(1)}, u32[]{:S(2)}, u32[]{:S(2)}) %all-to-all-start.1) | async-done | bytes 114720 | tf_op jit(solution)/shard_map/all_to_all | solution.py:280
  40.1 0.0 copy-done.1
  40.1 0.0 copy-start
  40.1 0.6 copy-done
  40.7 2.1 %score_tile.1 = (f32[16,2,896]{2,1,0:T(2,128)}, f32[32,2,768]{2,1,0:T(2,128)}) custom-call(bf16[32,2,896]{2,1,0:T(2,128)(2,1)} %copy-done, bf16[16,2,768]{2,1,0:T(2,128)(2,1)} %copy-done.1, s32[1,32]{1,0:T(1,128)} %fusion.id_ref, f32[1]{0:T(128)} %copy.11.scale_ref, f32[1]{0:T(128)S(6)} %copy.12.bias_ref), custom_call_target="tpu_custom_call" | custom-call | tf_op jit(solution)/shard_map/score_tile/pallas_call | solution.py:208
  42.8 16.1 %all_to_all.20.parts_ref = f32[16,2,896]{2,1,0:T(2,128)} all-to-all(f32[16,2,896]{2,1,0:T(2,128)} %get-tuple-element.18), channel_id=1, replica_groups=mesh['x'=4,'y_lo'=2,'core'=2,'z'=8,'y_hi'=4] {'y_hi','y_lo','core'}, dimensions={0} | all-to-all | bytes 229376 | tf_op jit(solution)/shard_map/all_to_all | solution.py:285
  59.0 3.9 %all-to-all-start.3 = ((f32[32,2,768]{2,1,0:T(2,128)}), f32[32,2,768]{2,1,0:T(2,128)S(1)}, u32[]{:S(2)}, u32[]{:S(2)}) async-start(f32[32,2,768]{2,1,0:T(2,128)} %get-tuple-element.19), calls=%async_computation.3 | async-start | bytes 393216 | tf_op jit(solution)/shard_map/all_to_all | solution.py:287
  62.8 0.8 %slice_reduce_fusion = f32[2]{0:T(128)S(1)} fusion(f32[2,128]{1,0:T(2,128)} %get-tuple-element.21), kind=kLoop, calls=%fused_computation.17 | loop fusion | bytes 16 | tf_op jit(solution)/shard_map/slice | solution.py:289
  63.6 1.7 %finish_text.1 = (f32[2,768]{1,0:T(2,128)}, f32[3]{0:T(128)}) custom-call(f32[16,2,896]{2,1,0:T(2,128)} %all_to_all.20.parts_ref, bf16[2,768]{1,0:T(2,128)(2,1)} %text_ref.1, f32[1]{0:T(128)} %copy.11.scale_ref), custom_call_target="tpu_custom_call" | custom-call | tf_op jit(solution)/shard_map/finish_text/pallas_call | solution.py:242
  65.3 7.7 %all-to-all-done.3 = f32[32,2,768]{2,1,0:T(2,128)S(1)} async-done(((f32[32,2,768]{2,1,0:T(2,128)}), f32[32,2,768]{2,1,0:T(2,128)S(1)}, u32[]{:S(2)}, u32[]{:S(2)}) %all-to-all-start.3) | async-done | bytes 196640 | tf_op jit(solution)/shard_map/all_to_all | solution.py:287
  73.0 0.1 reduce_sum.18
  73.1 0.8 %multiply_reduce_fusion = f32[2]{0:T(128)S(1)} fusion(f32[2,768]{1,0:T(2,128)} %get-tuple-element.20, f32[2,768]{1,0:T(2,128)S(1)} %reduce_sum.18, f32[]{:T(128)} %bitcast.1), kind=kLoop, calls=%fused_computation.1 | loop fusion | flops 4606 | bytes 12300 | tf_op jit(solution)/shard_map/reduce_sum | solution.py:170
  73.9 1.4 %subtract_multiply_fusion = f32[2,768]{1,0:T(2,128)} fusion(f32[2,768]{1,0:T(2,128)} %get-tuple-element.20, f32[2,768]{1,0:T(2,128)S(1)} %reduce_sum.18, f32[2]{0:T(128)S(1)} %slice_reduce_fusion, f32[2]{0:T(128)S(1)} %multiply_reduce_fusion, f32[]{:T(128)} %bitcast.2), kind=kLoop, calls=%fused_computation | loop fusion | flops 6144 | bytes 18452 | tf_op jit(solution)/shard_map/mul | solution.py:170
Async XLA Ops:
  2.0 17.6 %all-to-all-start = ((bf16[16,2,768]{2,1,0:T(2,128)(2,1)}), bf16[16,2,768]{2,1,0:T(2,128)(2,1)S(1)}, u32[]{:S(2)}, u32[]{:S(2)}) async-start(bf16[16,2,768]{2,1,0:T(2,128)(2,1)} %broadcast_in_dim.2), calls=%async_computation | async-start | bytes 98304 | tf_op jit(solution)/shard_map/all_to_all | solution.py:274
  19.6 20.4 %copy-start.1 = (bf16[16,2,768]{2,1,0:T(2,128)(2,1)}, bf16[16,2,768]{2,1,0:T(2,128)(2,1)S(1)}, u32[]{:S(2)}) copy-start(bf16[16,2,768]{2,1,0:T(2,128)(2,1)S(1)} %all-to-all-done.text_ref) | copy-start | bytes 147460
  19.6 20.4 %all-to-all-start.1 = ((bf16[32,2,896]{2,1,0:T(2,128)(2,1)}), bf16[32,2,896]{2,1,0:T(2,128)(2,1)S(1)}, u32[]{:S(2)}, u32[]{:S(2)}) async-start(bf16[32,2,896]{2,1,0:T(2,128)(2,1)} %get-tuple-element.15), calls=%async_computation.1 | async-start | bytes 229376 | tf_op jit(solution)/shard_map/all_to_all | solution.py:280
  40.1 0.6 copy-start
  59.0 14.0 %all-to-all-start.3 = ((f32[32,2,768]{2,1,0:T(2,128)}), f32[32,2,768]{2,1,0:T(2,128)S(1)}, u32[]{:S(2)}, u32[]{:S(2)}) async-start(f32[32,2,768]{2,1,0:T(2,128)} %get-tuple-element.19), calls=%async_computation.3 | async-start | bytes 393216 | tf_op jit(solution)/shard_map/all_to_all | solution.py:287

commit v2 on v0

--- a/solution.py
+++ b/solution.py
@@ -170,36 +170,51 @@
     return (direction - unit * jnp.sum(unit * direction, axis=-1, keepdims=True)) * inverse
 
 
-def text_kernel(text_ref, block_ref, unit_ref, inv_ref):
-    unit, inverse = unit_rows(text_ref[...].astype(jnp.float32))
-    block_ref[...] = jnp.broadcast_to(unit.astype(jnp.bfloat16)[None], block_ref.shape)
-    unit_ref[...] = unit
-    inv_ref[...] = jnp.broadcast_to(inverse, inv_ref.shape)
+def text_kernel(text_ref, block_ref):
+    unit, _ = unit_rows(text_ref[...].astype(jnp.float32))
+    unit = unit.astype(jnp.bfloat16)
+    for member in range(block_ref.shape[0]):
+        block_ref[member] = unit
 
 
 def text_blocks(text_embed, copies):
-    rows = text_embed.shape[0]
     vmem = pl.BlockSpec(memory_space=pltpu.VMEM)
     return pl.pallas_call(
         text_kernel,
-        out_shape=(
-            jax.ShapeDtypeStruct((copies,) + text_embed.shape, jnp.bfloat16),
-            jax.ShapeDtypeStruct(text_embed.shape, jnp.float32),
-            jax.ShapeDtypeStruct((rows, 128), jnp.float32),
-        ),
+        out_shape=jax.ShapeDtypeStruct((copies,) + text_embed.shape, jnp.bfloat16),
         in_specs=[vmem],
-        out_specs=(vmem, vmem, vmem),
+        out_specs=vmem,
         name="text_blocks",
     )(text_embed)
 
 
-def finish_kernel(total_tokens, parts_ref, unit_ref, inv_ref, scale_ref, grad_ref, scalar_ref):
-    feat_width = unit_ref.shape[-1]
+def image_part_kernel(grad_ref, text_ref, part_ref):
+    part = jnp.dot(grad_ref[...], text_ref[...], preferred_element_type=jnp.float32)
+    pair_count = part_ref.shape[1]
+    for member in range(part_ref.shape[0]):
+        part_ref[member] = part[member * pair_count : (member + 1) * pair_count]
+
+
+def image_parts(grad_bf, group_text, members):
+    vmem = pl.BlockSpec(memory_space=pltpu.VMEM)
+    pair_count = grad_bf.shape[0] // members
+    return pl.pallas_call(
+        image_part_kernel,
+        out_shape=jax.ShapeDtypeStruct((members, pair_count, group_text.shape[1]), jnp.float32),
+        in_specs=[vmem, vmem],
+        out_specs=vmem,
+        name="image_parts",
+    )(grad_bf, group_text)
+
+
+def finish_kernel(total_tokens, parts_ref, text_ref, scale_ref, grad_ref, scalar_ref):
+    feat_width = text_ref.shape[-1]
     total = parts_ref[0]
     for member in range(1, parts_ref.shape[0]):
         total = total + parts_ref[member]
     direction = scale_ref[0] * total[:, :feat_width]
-    grad_ref[...] = tangent(direction, unit_ref[...], inv_ref[...][:, :1])
+    unit, inverse = unit_rows(text_ref[...].astype(jnp.float32))
+    grad_ref[...] = tangent(direction, unit, inverse)
     side = total[:1, feat_width:]
     means = side[:, :32] + side[:, 32:64] + side[:, 64:96]
     means = means * (1.0 / total_tokens)
@@ -211,19 +226,19 @@
     scalar_ref[2] = jnp.sum(jnp.where(place < BITS, spread, 0.0))
 
 
-def finish_text(parts, text_unit, text_inv, logit_scale, total_tokens):
+def finish_text(parts, text_embed, logit_scale, total_tokens):
     vmem = pl.BlockSpec(memory_space=pltpu.VMEM)
     smem = pl.BlockSpec(memory_space=pltpu.SMEM)
     return pl.pallas_call(
         functools.partial(finish_kernel, total_tokens),
         out_shape=(
-            jax.ShapeDtypeStruct(text_unit.shape, jnp.float32),
+            jax.ShapeDtypeStruct(text_embed.shape, jnp.float32),
             jax.ShapeDtypeStruct((3,), jnp.float32),
         ),
-        in_specs=[vmem, vmem, vmem, smem],
+        in_specs=[vmem, vmem, smem],
         out_specs=(vmem, smem),
         name="finish_text",
-    )(parts, text_unit, text_inv, logit_scale)
+    )(parts, text_embed, logit_scale)
 
 
 def group_ids(sizes, axes, pair_count):
@@ -248,8 +263,7 @@
     scale_value = logit_scale[0]
     bias_value = logit_bias[0]
 
-    text_block, text_unit, text_inv = text_blocks(text_embed, n_text)
-    group_text = lax.all_to_all(text_block, TEXT_AXES, 0, 0)
+    group_text = lax.all_to_all(text_blocks(text_embed, n_text), TEXT_AXES, 0, 0)
 
     image_block, image_unit, image_inv = embed_images(
         latent, w_post, w_proj, gain, labels, n_image
@@ -277,13 +291,12 @@
     text_part = text_part.reshape(n_text, pair_count, feat_width + SIDE)
     text_part = lax.all_to_all(text_part, TEXT_AXES, 0, 0)
 
-    image_part = jnp.dot(grad_bf, group_text, preferred_element_type=jnp.float32)
-    image_part = image_part.reshape(n_image, pair_count, feat_width)
+    image_part = image_parts(grad_bf, group_text, n_image)
     image_part, text_part = lax.optimization_barrier((image_part, text_part))
     image_part = lax.all_to_all(image_part, IMAGE_AXES, 0, 0)
     image_dir = scale_value * jnp.sum(image_part, axis=0)
     grad_image = tangent(image_dir, image_unit, image_inv[:, :1])
-    grad_text, scalars = finish_text(text_part, text_unit, text_inv, logit_scale, total_tokens)
+    grad_text, scalars = finish_text(text_part, text_embed, logit_scale, total_tokens)
     return (grad_image, grad_text, scalars)
 
 

time: 73.9 us -> 73.1 us (0.989)
  Pallas kernels: 9.03 us -> 10.7 us
  waiting for transfers between devices: 26.3 us -> 24.8 us
  local copies, waits for them, and re-layouts: 1.96 us -> 1.04 us
    pallas_call x1 -> x2, Pallas kernels: 1.41 us -> 3.06 us  [the longest x1 1.65 us: image_parts(): pl.pallas_call(image_part_kernel, out_shape=jax.ShapeDtypeStruct((members...]
    all_to_all x1, waiting for transfers between devices: 8.69 us -> 7.16 us  [body(): text_part = lax.all_to_all(text_part, TEXT_AXES, 0, 0)]
    optimization_barrier x1 -> x0, local copies, waits for them, and re-layouts: 0.82 us -> none  [body(): image_part, text_part = lax.optimization_barrier((image_part, text_part))]
  transfers between devices with their start and end apart: 4 -> 4, of which waited for: 4 -> 4; matrix products, arithmetic and copies ran while one was open for 0% -> 0% of each run, Pallas kernels for 10% -> 13%
where the time goes in v2:
time: 73.1 us; the launch traced here: 72.5 us
  starting transfers between devices  32.5 us (44%)
  waiting for transfers between devices  24.8 us (34%)
  Pallas kernels  10.7 us (15%)
  between operations  2.08 us (3%)
  local copies, waits for them, and re-layouts  1.04 us (1%)
  other arithmetic  1.04 us (1%)
    all_to_all x1, starting transfers between devices, body(): group_block = lax.all_to_all(image_block, IMAGE_AXES, 0, 0)  11.3 us
    all_to_all x1, starting transfers between devices, body(): lax.all_to_all(text_blocks(text_embed, n_text), TEXT_AXES, 0, 0)  10.2 us
    all_to_all x1, waiting for transfers between devices, body(): image_part = lax.all_to_all(image_part, IMAGE_AXES, 0, 0)  8.34 us
    all_to_all x1, waiting for transfers between devices, body(): group_block = lax.all_to_all(image_block, IMAGE_AXES, 0, 0)  7.73 us
    all_to_all x1, starting transfers between devices, body(): text_part = lax.all_to_all(text_part, TEXT_AXES, 0, 0)  7.21 us
    all_to_all x1, waiting for transfers between devices, body(): text_part = lax.all_to_all(text_part, TEXT_AXES, 0, 0)  7.16 us
    pallas_call x1, Pallas kernels, embed_images(): pl.pallas_call(functools.partial(image_kernel, copies), out_shape=(jax.Sh...  5.93 us
    all_to_all x1, starting transfers between devices, body(): image_part = lax.all_to_all(image_part, IMAGE_AXES, 0, 0)  3.87 us
  transfers between devices with their start and end apart: 4, of which 4 were waited for; matrix products, arithmetic and copies ran while one was open for 0% of the time, Pallas kernels for 13%

profile of v2, /device:TPU:1, one launch (start us, length us, event | category | flops | bytes accessed | tf_op | source)
XLA Modules:
  0.0 72.5 jit_solution(5855105136401112833)
XLA Ops:
  0.6 1.4 %text_blocks.1 = bf16[16,2,768]{2,1,0:T(2,128)(2,1)} custom-call(bf16[2,768]{1,0:T(2,128)(2,1)} %text_ref.3), custom_call_target="tpu_custom_call" | custom-call | tf_op jit(solution)/shard_map/text_blocks/pallas_call | solution.py:182
  2.0 10.2 %all-to-all-start = ((bf16[16,2,768]{2,1,0:T(2,128)(2,1)}), bf16[16,2,768]{2,1,0:T(2,128)(2,1)S(1)}, u32[]{:S(2)}, u32[]{:S(2)}) async-start(bf16[16,2,768]{2,1,0:T(2,128)(2,1)} %text_blocks.1), calls=%async_computation | async-start | bytes 98304 | tf_op jit(solution)/shard_map/all_to_all | solution.py:266
  12.2 5.9 %embed_images.1 = (bf16[32,2,896]{2,1,0:T(2,128)(2,1)}, f32[2,768]{1,0:T(2,128)}, f32[2,128]{1,0:T(2,128)}) custom-call(f32[28,1024]{1,0:T(8,128)} %latent_hbm.1, bf16[28,1024]{1,0:T(8,128)(2,1)} %post_hbm.1, bf16[1024,768]{1,0:T(8,128)(2,1)} %proj_hbm.1, f32[768]{0:T(1024)} %gain_ref.1, s32[2]{0:T(128)} %label_ref.1), custom_call_target="tpu_custom_call" | custom-call | flops 2200000000 | bytes 1800000 | tf_op jit(solution)/shard_map/embed_images/pallas_call | solution.py:141
  18.1 0.0 copy-start.4
  18.2 0.0 copy-start.3
  18.2 1.5 %all-to-all-done = bf16[16,2,768]{2,1,0:T(2,128)(2,1)S(1)} async-done(((bf16[16,2,768]{2,1,0:T(2,128)(2,1)}), bf16[16,2,768]{2,1,0:T(2,128)(2,1)S(1)}, u32[]{:S(2)}, u32[]{:S(2)}) %all-to-all-start) | async-done | bytes 49184 | tf_op jit(solution)/shard_map/all_to_all | solution.py:266
  19.7 11.3 %all-to-all-start.1 = ((bf16[32,2,896]{2,1,0:T(2,128)(2,1)}), bf16[32,2,896]{2,1,0:T(2,128)(2,1)S(1)}, u32[]{:S(2)}, u32[]{:S(2)}) async-start(bf16[32,2,896]{2,1,0:T(2,128)(2,1)} %get-tuple-element.13), calls=%async_computation.1 | async-start | bytes 229376 | tf_op jit(solution)/shard_map/all_to_all | solution.py:273
  32.4 0.0 copy-start.1
  32.4 7.7 %all-to-all-done.1 = bf16[32,2,896]{2,1,0:T(2,128)(2,1)S(1)} async-done(((bf16[32,2,896]{2,1,0:T(2,128)(2,1)}), bf16[32,2,896]{2,1,0:T(2,128)(2,1)S(1)}, u32[]{:S(2)}, u32[]{:S(2)}) %all-to-all-start.1) | async-done | bytes 114720 | tf_op jit(solution)/shard_map/all_to_all | solution.py:273
  40.2 0.1 copy.16
  40.3 0.1 convert_reduce_fusion
  40.5 0.2 fusion.6.grad_ref
  40.6 0.0 copy-start.2
  40.6 0.2 fusion.7
  40.9 0.7 reshape.113
  41.6 7.2 %all-to-all-start.2 = ((f32[16,2,896]{2,1,0:T(2,128)}), f32[16,2,896]{2,1,0:T(2,128)S(1)}, u32[]{:S(2)}, u32[]{:S(2)}) async-start(f32[16,2,896]{2,1,0:T(2,128)} %reshape.113), calls=%async_computation.2 | async-start | bytes 229376 | tf_op jit(solution)/shard_map/all_to_all | solution.py:292
  48.8 0.0 copy-done.1
  48.8 0.0 copy-done.2
  48.8 1.6 %image_parts.1 = f32[32,2,768]{2,1,0:T(2,128)} custom-call(bf16[64,32]{1,0:T(8,128)(2,1)} %copy-done.2, bf16[32,768]{1,0:T(8,128)(2,1)} %copy-done.1), custom_call_target="tpu_custom_call" | custom-call | tf_op jit(solution)/shard_map/image_parts/pallas_call | solution.py:201
  50.4 7.2 %all-to-all-done.2.parts_ref = f32[16,2,896]{2,1,0:T(2,128)S(1)} async-done(((f32[16,2,896]{2,1,0:T(2,128)}), f32[16,2,896]{2,1,0:T(2,128)S(1)}, u32[]{:S(2)}, u32[]{:S(2)}) %all-to-all-start.2) | async-done | bytes 114720 | tf_op jit(solution)/shard_map/all_to_all | solution.py:292
  57.6 0.0 copy-start
  57.6 3.9 %all-to-all-start.3 = ((f32[32,2,768]{2,1,0:T(2,128)}), f32[32,2,768]{2,1,0:T(2,128)S(1)}, u32[]{:S(2)}, u32[]{:S(2)}) async-start(f32[32,2,768]{2,1,0:T(2,128)} %image_parts.1), calls=%async_computation.3 | async-start | bytes 393216 | tf_op jit(solution)/shard_map/all_to_all | solution.py:296
  61.5 0.0 copy-done.4
  61.5 0.1 slice_reduce_fusion
  61.6 0.0 copy-done
  61.6 1.7 %finish_text.1 = (f32[2,768]{1,0:T(2,128)}, f32[3]{0:T(128)}) custom-call(f32[16,2,896]{2,1,0:T(2,128)} %copy-done, bf16[2,768]{1,0:T(2,128)(2,1)} %text_ref.3, f32[1]{0:T(128)} %copy.17.scale_ref), custom_call_target="tpu_custom_call" | custom-call | tf_op jit(solution)/shard_map/finish_text/pallas_call | solution.py:232
  63.3 8.3 %all-to-all-done.3 = f32[32,2,768]{2,1,0:T(2,128)S(1)} async-done(((f32[32,2,768]{2,1,0:T(2,128)}), f32[32,2,768]{2,1,0:T(2,128)S(1)}, u32[]{:S(2)}, u32[]{:S(2)}) %all-to-all-start.3) | async-done | bytes 196640 | tf_op jit(solution)/shard_map/all_to_all | solution.py:296
  71.6 0.1 reduce_sum.28
  71.7 0.0 copy-done.3
  71.7 0.1 multiply_reduce_fusion
  71.9 0.7 subtract_multiply_fusion
  (8 shorter events, 0.1 us)
Async XLA Ops:
  2.0 17.7 %all-to-all-start = ((bf16[16,2,768]{2,1,0:T(2,128)(2,1)}), bf16[16,2,768]{2,1,0:T(2,128)(2,1)S(1)}, u32[]{:S(2)}, u32[]{:S(2)}) async-start(bf16[16,2,768]{2,1,0:T(2,128)(2,1)} %text_blocks.1), calls=%async_computation | async-start | bytes 98304 | tf_op jit(solution)/shard_map/all_to_all | solution.py:266
  18.1 43.3 %copy-start.4 = (f32[2,128]{1,0:T(2,128)S(1)}, f32[2,128]{1,0:T(2,128)}, u32[]{:S(2)}) copy-start(f32[2,128]{1,0:T(2,128)} %get-tuple-element.17) | copy-start | bytes 3076
  18.2 53.6 %copy-start.3 = (f32[2,768]{1,0:T(2,128)S(1)}, f32[2,768]{1,0:T(2,128)}, u32[]{:S(2)}) copy-start(f32[2,768]{1,0:T(2,128)} %get-tuple-element.16) | copy-start | bytes 18436
  19.7 20.4 %all-to-all-start.1 = ((bf16[32,2,896]{2,1,0:T(2,128)(2,1)}), bf16[32,2,896]{2,1,0:T(2,128)(2,1)S(1)}, u32[]{:S(2)}, u32[]{:S(2)}) async-start(bf16[32,2,896]{2,1,0:T(2,128)(2,1)} %get-tuple-element.13), calls=%async_computation.1 | async-start | bytes 229376 | tf_op jit(solution)/shard_map/all_to_all | solution.py:273
  32.4 16.4 %copy-start.1 = (bf16[32,768]{1,0:T(8,128)(2,1)}, bf16[32,768]{1,0:T(8,128)(2,1)S(1)}, u32[]{:S(2)}) copy-start(bf16[32,768]{1,0:T(8,128)(2,1)S(1)} %reshape.112.text_ref) | copy-start | bytes 147460
  40.6 8.1 %copy-start.2 = (bf16[64,32]{1,0:T(8,128)(2,1)}, bf16[64,32]{1,0:T(8,128)(2,1)S(1)}, u32[]{:S(2)}) copy-start(bf16[64,32]{1,0:T(8,128)(2,1)S(1)} %fusion.6.grad_ref) | copy-start | bytes 12292
  41.6 16.0 %all-to-all-start.2 = ((f32[16,2,896]{2,1,0:T(2,128)}), f32[16,2,896]{2,1,0:T(2,128)S(1)}, u32[]{:S(2)}, u32[]{:S(2)}) async-start(f32[16,2,896]{2,1,0:T(2,128)} %reshape.113), calls=%async_computation.2 | async-start | bytes 229376 | tf_op jit(solution)/shard_map/all_to_all | solution.py:292
  57.6 4.0 %copy-start = (f32[16,2,896]{2,1,0:T(2,128)}, f32[16,2,896]{2,1,0:T(2,128)S(1)}, u32[]{:S(2)}) copy-start(f32[16,2,896]{2,1,0:T(2,128)S(1)} %all-to-all-done.2.parts_ref) | copy-start | bytes 344068
  57.6 14.0 %all-to-all-start.3 = ((f32[32,2,768]{2,1,0:T(2,128)}), f32[32,2,768]{2,1,0:T(2,128)S(1)}, u32[]{:S(2)}, u32[]{:S(2)}) async-start(f32[32,2,768]{2,1,0:T(2,128)} %image_parts.1), calls=%async_computation.3 | async-start | bytes 393216 | tf_op jit(solution)/shard_map/all_to_all | solution.py:296

commit v3 on v2

--- a/solution.py
+++ b/solution.py
@@ -17,8 +17,8 @@
 
 ROW_AXES = ("x", "y_lo", "core")
 BLK_AXES = ("z", "y_hi")
-TEXT_AXES = ("y_hi", "y_lo", "core")
-IMAGE_AXES = ("x", "z")
+TEXT_AXES = ("x", "core")
+IMAGE_AXES = ("z", "y_hi", "y_lo")
 
 
 def code_sums(latent):
@@ -188,25 +188,6 @@
     )(text_embed)
 
 
-def image_part_kernel(grad_ref, text_ref, part_ref):
-    part = jnp.dot(grad_ref[...], text_ref[...], preferred_element_type=jnp.float32)
-    pair_count = part_ref.shape[1]
-    for member in range(part_ref.shape[0]):
-        part_ref[member] = part[member * pair_count : (member + 1) * pair_count]
-
-
-def image_parts(grad_bf, group_text, members):
-    vmem = pl.BlockSpec(memory_space=pltpu.VMEM)
-    pair_count = grad_bf.shape[0] // members
-    return pl.pallas_call(
-        image_part_kernel,
-        out_shape=jax.ShapeDtypeStruct((members, pair_count, group_text.shape[1]), jnp.float32),
-        in_specs=[vmem, vmem],
-        out_specs=vmem,
-        name="image_parts",
-    )(grad_bf, group_text)
-
-
 def finish_kernel(total_tokens, parts_ref, text_ref, scale_ref, grad_ref, scalar_ref):
     feat_width = text_ref.shape[-1]
     total = parts_ref[0]
@@ -241,35 +222,44 @@
     )(parts, text_embed, logit_scale)
 
 
-def group_ids(sizes, axes, pair_count):
-    count = math.prod(sizes[axis] for axis in axes)
-    member = jnp.arange(count * pair_count, dtype=jnp.int32) // pair_count
-    place = {axis: lax.axis_index(axis) for axis in ROW_AXES + BLK_AXES}
-    for axis in reversed(axes):
-        place[axis] = member % sizes[axis]
-        member = member // sizes[axis]
-    device = jnp.int32(0)
-    for axis in ROW_AXES + BLK_AXES:
-        device = device * sizes[axis] + place[axis]
-    return device * pair_count + jnp.arange(count * pair_count, dtype=jnp.int32) % pair_count
+def swap_cores(block):
+    return lax.ppermute(block, "core", [(0, 1), (1, 0)])
+
+
+def along_x(block, distance, count):
+    return lax.ppermute(block, "x", [(i, (i + distance) % count) for i in range(count)])
+
+
+def from_here(members, n_x):
+    members = members.reshape((n_x, 2) + members.shape[1:])
+    here = lax.axis_index("x")
+    other = lax.axis_index("core") == 1
+    turned = [
+        lax.dynamic_index_in_dim(members, (here + distance) % n_x, 0, keepdims=False)
+        for distance in range(n_x)
+    ]
+    return [
+        jnp.where(other, block[1 - core], block[core]) for block in turned for core in range(2)
+    ]
 
 
 def body(sizes, latent, w_post, w_proj, gain, text_embed, labels, logit_scale, logit_bias):
     pair_count, feat_width = text_embed.shape
+    n_x = sizes["x"]
     n_image = math.prod(sizes[axis] for axis in IMAGE_AXES)
     n_text = math.prod(sizes[axis] for axis in TEXT_AXES)
     text_count = n_text * pair_count
+    chip_count = 2 * pair_count
     total_tokens = latent.shape[1] * math.prod(sizes.values())
     scale_value = logit_scale[0]
     bias_value = logit_bias[0]
 
     group_text = lax.all_to_all(text_blocks(text_embed, n_text), TEXT_AXES, 0, 0)
+    group_text = jnp.concatenate(from_here(group_text, n_x), axis=0)
 
     image_block, image_unit, image_inv = embed_images(
         latent, w_post, w_proj, gain, labels, n_image
     )
-    image_block, group_text = lax.optimization_barrier((image_block, group_text))
-    group_text = group_text.reshape(text_count, feat_width)
     group_block = lax.all_to_all(image_block, IMAGE_AXES, 0, 0)
     group_block = group_block.reshape(n_image * pair_count, feat_width + SIDE)
     group_image = group_block[:, :feat_width]
@@ -277,26 +267,38 @@
     group_labels = (group_side[:, SIDE - 2] * 32.0 + group_side[:, SIDE - 1]).astype(jnp.int32)
     group_sums = jnp.sum(group_side, axis=0, keepdims=True)
 
-    text_ids = group_ids(sizes, TEXT_AXES, pair_count)
+    row_size = sizes["y_lo"] * sizes["core"]
+    blk_size = sizes["z"] * sizes["y_hi"]
+    place = jnp.arange(text_count, dtype=jnp.int32)
+    text_x = (lax.axis_index("x") + place // chip_count) % n_x
+    text_core = lax.axis_index("core") ^ (place // pair_count % 2)
+    text_row = text_x * row_size + lax.axis_index("y_lo") * sizes["core"] + text_core
+    text_blk = lax.axis_index("z") * sizes["y_hi"] + lax.axis_index("y_hi")
+    text_ids = (text_row * blk_size + text_blk) * pair_count + place % pair_count
+
     products = jnp.dot(group_image, group_text.T, preferred_element_type=jnp.float32)
     pair_sign = jnp.where(
         group_labels[:, None] == text_ids[None, :], jnp.float32(1.0), jnp.float32(-1.0)
     )
     margin = pair_sign * (scale_value * products + bias_value)
     grad_bf = (-pair_sign * jax.nn.sigmoid(-margin)).astype(jnp.bfloat16)
+    image_part = jnp.dot(grad_bf, group_text, preferred_element_type=jnp.float32)
+    image_part = image_part.reshape(n_image, pair_count, feat_width)
+    image_part = lax.all_to_all(image_part, IMAGE_AXES, 0, 0)
+
     text_part = jnp.dot(grad_bf.T, group_image, preferred_element_type=jnp.float32)
     text_part = jnp.concatenate(
         [text_part, jnp.broadcast_to(group_sums, (text_count, SIDE))], axis=1
     )
-    text_part = text_part.reshape(n_text, pair_count, feat_width + SIDE)
-    text_part = lax.all_to_all(text_part, TEXT_AXES, 0, 0)
-
-    image_part = image_parts(grad_bf, group_text, n_image)
-    image_part, text_part = lax.optimization_barrier((image_part, text_part))
-    image_part = lax.all_to_all(image_part, IMAGE_AXES, 0, 0)
+    chip_part = text_part[:chip_count]
+    for distance in range(1, n_x):
+        rows = text_part[distance * chip_count : (distance + 1) * chip_count]
+        chip_part = chip_part + along_x(rows, distance, n_x)
+    text_part = chip_part[:pair_count] + swap_cores(chip_part[pair_count:])
+    grad_text, scalars = finish_text(text_part[None], text_embed, logit_scale, total_tokens)
+
     image_dir = scale_value * jnp.sum(image_part, axis=0)
     grad_image = tangent(image_dir, image_unit, image_inv[:, :1])
-    grad_text, scalars = finish_text(text_part, text_embed, logit_scale, total_tokens)
     return (grad_image, grad_text, scalars)
 
 

time: 73.1 us -> 72.6 us (level)
  waiting for transfers between devices: 24.8 us -> 15 us
  starting transfers between devices: 32.5 us -> 42.2 us
  Pallas kernels: 10.7 us -> 8.87 us
    ppermute x0 -> x4, starting transfers between devices: none -> 15.2 us  [the longest x3 10 us: along_x(): lax.ppermute(block, 'x', [(i, (i + distance) % count) for i in range(coun...]
    all_to_all x1, waiting for transfers between devices: 8.34 us -> 0.01 us  [body(): image_part = lax.all_to_all(image_part, IMAGE_AXES, 0, 0)]
    all_to_all x1 -> x0, starting transfers between devices: 7.21 us -> none  [body(): text_part = lax.all_to_all(text_part, TEXT_AXES, 0, 0)]
    all_to_all x1 -> x0, waiting for transfers between devices: 7.16 us -> none  [body(): text_part = lax.all_to_all(text_part, TEXT_AXES, 0, 0)]
    all_to_all x1, waiting for transfers between devices: 7.73 us -> 11.6 us  [body(): group_block = lax.all_to_all(image_block, IMAGE_AXES, 0, 0)]
    ppermute x0 -> x4, waiting for transfers between devices: none -> 3.4 us  [the longest x3 2.72 us: along_x(): lax.ppermute(block, 'x', [(i, (i + distance) % count) for i in range(coun...]
    pallas_call x1 -> x0, Pallas kernels: 1.65 us -> none  [image_parts(): pl.pallas_call(image_part_kernel, out_shape=jax.ShapeDtypeStruct((members...]
    all_to_all x1, waiting for transfers between devices: 1.55 us -> 0.01 us  [body(): lax.all_to_all(text_blocks(text_embed, n_text), TEXT_AXES, 0, 0)]
  transfers between devices with their start and end apart: 4 -> 7, of which waited for: 4 -> 3; matrix products, arithmetic and copies ran while one was open for 0% -> 1% of each run, Pallas kernels for 13% -> 10%
where the time goes in v3:
time: 72.6 us; the launch traced here: 72.1 us
  starting transfers between devices  42.2 us (58%)
  waiting for transfers between devices  15 us (21%)
  Pallas kernels  8.87 us (12%)
  between operations  2.2 us (3%)
  other arithmetic  1.75 us (2%)
  local copies, waits for them, and re-layouts  1.39 us (2%)
    all_to_all x1, starting transfers between devices, body(): group_block = lax.all_to_all(image_block, IMAGE_AXES, 0, 0)  12 us
    all_to_all x1, waiting for transfers between devices, body(): group_block = lax.all_to_all(image_block, IMAGE_AXES, 0, 0)  11.6 us
    all_to_all x1, starting transfers between devices, body(): lax.all_to_all(text_blocks(text_embed, n_text), TEXT_AXES, 0, 0)  10.1 us
    ppermute x3, starting transfers between devices, along_x(): lax.ppermute(block, 'x', [(i, (i + distance) % count) for i in range(coun...  10 us
    pallas_call x1, Pallas kernels, embed_images(): pl.pallas_call(functools.partial(image_kernel, copies), out_shape=(jax.Sh...  5.98 us
    ppermute x1, starting transfers between devices, swap_cores(): return lax.ppermute(block, 'core', [(0, 1), (1, 0)])  5.24 us
    all_to_all x1, starting transfers between devices, body(): image_part = lax.all_to_all(image_part, IMAGE_AXES, 0, 0)  4.87 us
    ppermute x3, waiting for transfers between devices, along_x(): lax.ppermute(block, 'x', [(i, (i + distance) % count) for i in range(coun...  2.72 us
  transfers between devices with their start and end apart: 7, of which 3 were waited for; matrix products, arithmetic and copies ran while one was open for 1% of the time, Pallas kernels for 10%

profile of v3, /device:TPU:1, one launch (start us, length us, event | category | flops | bytes accessed | tf_op | source)
XLA Modules:
  0.0 72.1 jit_solution(15065320387951556777)
XLA Ops:
  0.6 1.4 %text_blocks.1 = bf16[8,2,768]{2,1,0:T(2,128)(2,1)} custom-call(bf16[2,768]{1,0:T(2,128)(2,1)} %text_ref.3), custom_call_target="tpu_custom_call" | custom-call | tf_op jit(solution)/shard_map/text_blocks/pallas_call | solution.py:182
  2.0 10.1 %all-to-all-start.1 = ((bf16[8,2,768]{2,1,0:T(2,128)(2,1)}), bf16[8,2,768]{2,1,0:T(2,128)(2,1)S(1)}, u32[]{:S(2)}, u32[]{:S(2)}) async-start(bf16[8,2,768]{2,1,0:T(2,128)(2,1)} %text_blocks.1), calls=%async_computation.1 | async-start | bytes 49152 | tf_op jit(solution)/shard_map/all_to_all | solution.py:257
  12.1 6.0 %embed_images.1 = (bf16[64,2,896]{2,1,0:T(2,128)(2,1)}, f32[2,768]{1,0:T(2,128)}, f32[2,128]{1,0:T(2,128)}) custom-call(f32[28,1024]{1,0:T(8,128)} %latent_hbm.1, bf16[28,1024]{1,0:T(8,128)(2,1)} %post_hbm.1, bf16[1024,768]{1,0:T(8,128)(2,1)} %proj_hbm.1, f32[768]{0:T(1024)} %gain_ref.1, s32[2]{0:T(128)} %label_ref.1), custom_call_target="tpu_custom_call" | custom-call | flops 2200000000 | bytes 1800000 | tf_op jit(solution)/shard_map/embed_images/pallas_call | solution.py:141
  18.1 0.0 all-to-all-done.1
  18.1 12.0 %all-to-all-start = ((bf16[64,2,896]{2,1,0:T(2,128)(2,1)}), bf16[64,2,896]{2,1,0:T(2,128)(2,1)S(1)}, u32[]{:S(2)}, u32[]{:S(2)}) async-start(bf16[64,2,896]{2,1,0:T(2,128)(2,1)} %get-tuple-element.8), calls=%async_computation | async-start | bytes 458752 | tf_op jit(solution)/shard_map/all_to_all | solution.py:263
  31.6 0.1 concatenate.6
  31.6 11.6 %all-to-all-done = bf16[64,2,896]{2,1,0:T(2,128)(2,1)S(1)} async-done(((bf16[64,2,896]{2,1,0:T(2,128)(2,1)}), bf16[64,2,896]{2,1,0:T(2,128)(2,1)S(1)}, u32[]{:S(2)}, u32[]{:S(2)}) %all-to-all-start) | async-done | bytes 229408 | tf_op jit(solution)/shard_map/all_to_all | solution.py:263
  43.3 0.1 reshape.108
  43.4 0.0 copy-start.1
  43.4 0.1 copy.13
  43.5 0.1 convert_reduce_fusion
  43.7 0.0 copy-start
  43.7 0.2 fusion.6
  43.9 0.1 fusion.7
  44.0 0.2 fusion.35
  44.3 1.0 %reshape.110 = f32[64,2,768]{2,1,0:T(2,128)} reshape(f32[128,768]{1,0:T(8,128)S(1)} %fusion.35) | data formatting | bytes 786432 | tf_op jit(solution)/shard_map/reshape | solution.py:286
  45.2 4.9 %all-to-all-start.2 = ((f32[64,2,768]{2,1,0:T(2,128)}), f32[64,2,768]{2,1,0:T(2,128)S(1)}, u32[]{:S(2)}, u32[]{:S(2)}) async-start(f32[64,2,768]{2,1,0:T(2,128)} %reshape.110), calls=%async_computation.2 | async-start | bytes 786432 | tf_op jit(solution)/shard_map/all_to_all | solution.py:287
  50.2 3.2 %collective-permute-start = (f32[4,896]{1,0:T(4,128)S(1)}, f32[4,896]{1,0:T(4,128)S(1)}, u32[]{:S(2)}, u32[]{:S(2)}) collective-permute-start(f32[4,896]{1,0:T(4,128)S(1)} %get-tuple-element.13), channel_id=1, source_target_pairs={{0,128},{128,256},{256,384},{384,0},{1,129},{129,257},{257,385},{3... | collective-permute-start | bytes 43016 | tf_op jit(solution)/shard_map/ppermute | solution.py:230
  53.4 3.3 %collective-permute-start.2 = (f32[4,896]{1,0:T(4,128)S(1)}, f32[4,896]{1,0:T(4,128)S(1)}, u32[]{:S(2)}, u32[]{:S(2)}) collective-permute-start(f32[4,896]{1,0:T(4,128)S(1)} %get-tuple-element.14), channel_id=1, source_target_pairs={{0,384},{128,0},{256,128},{384,256},{1,385},{129,1},{257,129},{385... | collective-permute-start | bytes 43016 | tf_op jit(solution)/shard_map/ppermute | solution.py:230
  56.7 3.5 %collective-permute-start.1 = (f32[4,896]{1,0:T(4,128)S(1)}, f32[4,896]{1,0:T(4,128)S(1)}, u32[]{:S(2)}, u32[]{:S(2)}) collective-permute-start(f32[4,896]{1,0:T(4,128)S(1)} %get-tuple-element.15), channel_id=1, source_target_pairs={{0,256},{128,384},{256,0},{384,128},{1,257},{129,385},{257,1},{385... | collective-permute-start | bytes 43016 | tf_op jit(solution)/shard_map/ppermute | solution.py:230
  60.2 0.0 collective-permute-done
  60.2 0.0 collective-permute-done.2
  60.2 2.7 %collective-permute-done.1 = f32[4,896]{1,0:T(4,128)S(1)} collective-permute-done((f32[4,896]{1,0:T(4,128)S(1)}, f32[4,896]{1,0:T(4,128)S(1)}, u32[]{:S(2)}, u32[]{:S(2)}) %collective-permute-start.1) | collective-permute-done | bytes 14368 | tf_op jit(solution)/shard_map/ppermute | solution.py:230
  63.0 5.2 %collective-permute-start.3 = (f32[2,896]{1,0:T(2,128)S(1)}, f32[2,896]{1,0:T(2,128)S(1)}, u32[]{:S(2)}, u32[]{:S(2)}) collective-permute-start(f32[2,896]{1,0:T(2,128)S(1)} %slice.101), channel_id=1, source_target_pairs={{0,32},{32,0},{1,33},{33,1},{2,34},{34,2},{3,35},{35,3},{4,36},{36... | collective-permute-start | bytes 21512 | tf_op jit(solution)/shard_map/ppermute | solution.py:226
  68.2 0.0 copy-done.1
  68.2 0.1 slice_reduce_fusion
  68.3 0.7 collective-permute-done.3
  69.0 0.6 fusion.12.parts_ref
  69.6 1.5 %finish_text.1 = (f32[2,768]{1,0:T(2,128)}, f32[3]{0:T(128)}) custom-call(f32[1,2,896]{2,1,0:T(2,128)} %fusion.12.parts_ref, bf16[2,768]{1,0:T(2,128)(2,1)} %text_ref.3, f32[1]{0:T(128)} %copy.14.scale_ref), custom_call_target="tpu_custom_call" | custom-call | tf_op jit(solution)/shard_map/finish_text/pallas_call | solution.py:213
  71.1 0.0 all-to-all-done.2
  71.1 0.2 reduce_sum.27
  71.3 0.0 copy-done
  71.3 0.1 multiply_reduce_fusion
  71.4 0.7 subtract_multiply_fusion
  (10 shorter events, 0.1 us)
Async XLA Ops:
  2.0 16.1 %all-to-all-start.1 = ((bf16[8,2,768]{2,1,0:T(2,128)(2,1)}), bf16[8,2,768]{2,1,0:T(2,128)(2,1)S(1)}, u32[]{:S(2)}, u32[]{:S(2)}) async-start(bf16[8,2,768]{2,1,0:T(2,128)(2,1)} %text_blocks.1), calls=%async_computation.1 | async-start | bytes 49152 | tf_op jit(solution)/shard_map/all_to_all | solution.py:257
  18.1 25.1 %all-to-all-start = ((bf16[64,2,896]{2,1,0:T(2,128)(2,1)}), bf16[64,2,896]{2,1,0:T(2,128)(2,1)S(1)}, u32[]{:S(2)}, u32[]{:S(2)}) async-start(bf16[64,2,896]{2,1,0:T(2,128)(2,1)} %get-tuple-element.8), calls=%async_computation | async-start | bytes 458752 | tf_op jit(solution)/shard_map/all_to_all | solution.py:263
  43.4 24.8 %copy-start.1 = (f32[2,128]{1,0:T(2,128)S(1)}, f32[2,128]{1,0:T(2,128)}, u32[]{:S(2)}) copy-start(f32[2,128]{1,0:T(2,128)} %get-tuple-element.10) | copy-start | bytes 3076
  43.7 27.6 %copy-start = (f32[2,768]{1,0:T(2,128)S(1)}, f32[2,768]{1,0:T(2,128)}, u32[]{:S(2)}) copy-start(f32[2,768]{1,0:T(2,128)} %get-tuple-element.9) | copy-start | bytes 18436
  45.2 25.9 %all-to-all-start.2 = ((f32[64,2,768]{2,1,0:T(2,128)}), f32[64,2,768]{2,1,0:T(2,128)S(1)}, u32[]{:S(2)}, u32[]{:S(2)}) async-start(f32[64,2,768]{2,1,0:T(2,128)} %reshape.110), calls=%async_computation.2 | async-start | bytes 786432 | tf_op jit(solution)/shard_map/all_to_all | solution.py:287
  50.2 10.0 %collective-permute-start = (f32[4,896]{1,0:T(4,128)S(1)}, f32[4,896]{1,0:T(4,128)S(1)}, u32[]{:S(2)}, u32[]{:S(2)}) collective-permute-start(f32[4,896]{1,0:T(4,128)S(1)} %get-tuple-element.13), channel_id=1, source_target_pairs={{0,128},{128,256},{256,384},{384,0},{1,129},{129,257},{257,385},{3... | collective-permute-start | bytes 43016 | tf_op jit(solution)/shard_map/ppermute | solution.py:230
  53.4 6.8 %collective-permute-start.2 = (f32[4,896]{1,0:T(4,128)S(1)}, f32[4,896]{1,0:T(4,128)S(1)}, u32[]{:S(2)}, u32[]{:S(2)}) collective-permute-start(f32[4,896]{1,0:T(4,128)S(1)} %get-tuple-element.14), channel_id=1, source_target_pairs={{0,384},{128,0},{256,128},{384,256},{1,385},{129,1},{257,129},{385... | collective-permute-start | bytes 43016 | tf_op jit(solution)/shard_map/ppermute | solution.py:230
  56.7 6.3 %collective-permute-start.1 = (f32[4,896]{1,0:T(4,128)S(1)}, f32[4,896]{1,0:T(4,128)S(1)}, u32[]{:S(2)}, u32[]{:S(2)}) collective-permute-start(f32[4,896]{1,0:T(4,128)S(1)} %get-tuple-element.15), channel_id=1, source_target_pairs={{0,256},{128,384},{256,0},{384,128},{1,257},{129,385},{257,1},{385... | collective-permute-start | bytes 43016 | tf_op jit(solution)/shard_map/ppermute | solution.py:230
  63.0 6.1 %collective-permute-start.3 = (f32[2,896]{1,0:T(2,128)S(1)}, f32[2,896]{1,0:T(2,128)S(1)}, u32[]{:S(2)}, u32[]{:S(2)}) collective-permute-start(f32[2,896]{1,0:T(2,128)S(1)} %slice.101), channel_id=1, source_target_pairs={{0,32},{32,0},{1,33},{33,1},{2,34},{34,2},{3,35},{35,3},{4,36},{36... | collective-permute-start | bytes 21512 | tf_op jit(solution)/shard_map/ppermute | solution.py:226

commit v4 on v3

--- a/solution.py
+++ b/solution.py
@@ -188,11 +188,9 @@
     )(text_embed)
 
 
-def finish_kernel(total_tokens, parts_ref, text_ref, scale_ref, grad_ref, scalar_ref):
-    feat_width = text_ref.shape[-1]
-    total = parts_ref[0]
-    for member in range(1, parts_ref.shape[0]):
-        total = total + parts_ref[member]
+def finish_kernel(total_tokens, chip_ref, moved_ref, text_ref, scale_ref, grad_ref, scalar_ref):
+    pair_count, feat_width = text_ref.shape
+    total = chip_ref[:pair_count] + moved_ref[...]
     direction = scale_ref[0] * total[:, :feat_width]
     unit, inverse = unit_rows(text_ref[...].astype(jnp.float32))
     grad_ref[...] = tangent(direction, unit, inverse)
@@ -207,7 +205,7 @@
     scalar_ref[2] = jnp.sum(jnp.where(place < BITS, spread, 0.0))
 
 
-def finish_text(parts, text_embed, logit_scale, total_tokens):
+def finish_text(chip_part, moved, text_embed, logit_scale, total_tokens):
     vmem = pl.BlockSpec(memory_space=pltpu.VMEM)
     smem = pl.BlockSpec(memory_space=pltpu.SMEM)
     return pl.pallas_call(
@@ -216,10 +214,10 @@
             jax.ShapeDtypeStruct(text_embed.shape, jnp.float32),
             jax.ShapeDtypeStruct((3,), jnp.float32),
         ),
-        in_specs=[vmem, vmem, smem],
+        in_specs=[vmem, vmem, vmem, smem],
         out_specs=(vmem, smem),
         name="finish_text",
-    )(parts, text_embed, logit_scale)
+    )(chip_part, moved, text_embed, logit_scale)
 
 
 def swap_cores(block):
@@ -294,11 +292,12 @@
     for distance in range(1, n_x):
         rows = text_part[distance * chip_count : (distance + 1) * chip_count]
         chip_part = chip_part + along_x(rows, distance, n_x)
-    text_part = chip_part[:pair_count] + swap_cores(chip_part[pair_count:])
-    grad_text, scalars = finish_text(text_part[None], text_embed, logit_scale, total_tokens)
+    moved = swap_cores(chip_part[pair_count:])
 
     image_dir = scale_value * jnp.sum(image_part, axis=0)
     grad_image = tangent(image_dir, image_unit, image_inv[:, :1])
+    grad_image, moved = lax.optimization_barrier((grad_image, moved))
+    grad_text, scalars = finish_text(chip_part, moved, text_embed, logit_scale, total_tokens)
     return (grad_image, grad_text, scalars)
 
 

time: 72.6 us -> 71.9 us (level)
  waiting for transfers between devices: 15 us -> 14.2 us
  transfers between devices with their start and end apart: 7 -> 7, of which waited for: 3 -> 2; matrix products, arithmetic and copies ran while one was open for 1% -> 2% of each run, Pallas kernels for 10% -> 8%
where the time goes in v4:
time: 71.9 us; the launch traced here: 71.3 us
  starting transfers between devices  42.3 us (59%)
  waiting for transfers between devices  14.2 us (20%)
  Pallas kernels  8.91 us (12%)
  between operations  2.2 us (3%)
  local copies, waits for them, and re-layouts  2.01 us (3%)
  other arithmetic  1.16 us (2%)
    all_to_all x1, starting transfers between devices, body(): group_block = lax.all_to_all(image_block, IMAGE_AXES, 0, 0)  12 us
    all_to_all x1, waiting for transfers between devices, body(): group_block = lax.all_to_all(image_block, IMAGE_AXES, 0, 0)  11.6 us
    all_to_all x1, starting transfers between devices, body(): lax.all_to_all(text_blocks(text_embed, n_text), TEXT_AXES, 0, 0)  10.1 us
    ppermute x3, starting transfers between devices, along_x(): lax.ppermute(block, 'x', [(i, (i + distance) % count) for i in range(coun...  10 us
    pallas_call x1, Pallas kernels, embed_images(): pl.pallas_call(functools.partial(image_kernel, copies), out_shape=(jax.Sh...  5.98 us
    ppermute x1, starting transfers between devices, swap_cores(): return lax.ppermute(block, 'core', [(0, 1), (1, 0)])  5.25 us
    all_to_all x1, starting transfers between devices, body(): image_part = lax.all_to_all(image_part, IMAGE_AXES, 0, 0)  4.87 us
    ppermute x3, waiting for transfers between devices, along_x(): lax.ppermute(block, 'x', [(i, (i + distance) % count) for i in range(coun...  2.59 us
  transfers between devices with their start and end apart: 7, of which 2 were waited for; matrix products, arithmetic and copies ran while one was open for 2% of the time, Pallas kernels for 8%

profile of v4, /device:TPU:1, one launch (start us, length us, event | category | flops | bytes accessed | tf_op | source)
XLA Modules:
  0.0 71.3 jit_solution(17593659187922554463)
XLA Ops:
  0.6 1.4 %text_blocks.1 = bf16[8,2,768]{2,1,0:T(2,128)(2,1)} custom-call(bf16[2,768]{1,0:T(2,128)(2,1)} %text_ref.3), custom_call_target="tpu_custom_call" | custom-call | tf_op jit(solution)/shard_map/text_blocks/pallas_call | solution.py:182
  2.0 10.1 %all-to-all-start.1 = ((bf16[8,2,768]{2,1,0:T(2,128)(2,1)}), bf16[8,2,768]{2,1,0:T(2,128)(2,1)S(1)}, u32[]{:S(2)}, u32[]{:S(2)}) async-start(bf16[8,2,768]{2,1,0:T(2,128)(2,1)} %text_blocks.1), calls=%async_computation.1 | async-start | bytes 49152 | tf_op jit(solution)/shard_map/all_to_all | solution.py:255
  12.1 6.0 %embed_images.1 = (bf16[64,2,896]{2,1,0:T(2,128)(2,1)}, f32[2,768]{1,0:T(2,128)}, f32[2,128]{1,0:T(2,128)}) custom-call(f32[28,1024]{1,0:T(8,128)} %latent_hbm.1, bf16[28,1024]{1,0:T(8,128)(2,1)} %post_hbm.1, bf16[1024,768]{1,0:T(8,128)(2,1)} %proj_hbm.1, f32[768]{0:T(1024)} %gain_ref.1, s32[2]{0:T(128)} %label_ref.1), custom_call_target="tpu_custom_call" | custom-call | flops 2200000000 | bytes 1800000 | tf_op jit(solution)/shard_map/embed_images/pallas_call | solution.py:141
  18.1 0.0 all-to-all-done.1
  18.1 12.0 %all-to-all-start = ((bf16[64,2,896]{2,1,0:T(2,128)(2,1)}), bf16[64,2,896]{2,1,0:T(2,128)(2,1)S(1)}, u32[]{:S(2)}, u32[]{:S(2)}) async-start(bf16[64,2,896]{2,1,0:T(2,128)(2,1)} %get-tuple-element.10), calls=%async_computation | async-start | bytes 458752 | tf_op jit(solution)/shard_map/all_to_all | solution.py:261
  31.6 0.1 concatenate.6
  31.6 11.6 %all-to-all-done = bf16[64,2,896]{2,1,0:T(2,128)(2,1)S(1)} async-done(((bf16[64,2,896]{2,1,0:T(2,128)(2,1)}), bf16[64,2,896]{2,1,0:T(2,128)(2,1)S(1)}, u32[]{:S(2)}, u32[]{:S(2)}) %all-to-all-start) | async-done | bytes 229408 | tf_op jit(solution)/shard_map/all_to_all | solution.py:261
  43.3 0.1 reshape.108
  43.3 0.0 copy-start.3
  43.4 0.1 copy.13
  43.5 0.1 convert_reduce_fusion
  43.6 0.0 copy-start.1
  43.6 0.2 fusion.6
  43.8 0.1 fusion.7
  44.0 0.2 fusion.34
  44.2 1.0 %reshape.110 = f32[64,2,768]{2,1,0:T(2,128)} reshape(f32[128,768]{1,0:T(8,128)S(1)} %fusion.34) | data formatting | bytes 786432 | tf_op jit(solution)/shard_map/reshape | solution.py:284
  45.2 4.9 %all-to-all-start.2 = ((f32[64,2,768]{2,1,0:T(2,128)}), f32[64,2,768]{2,1,0:T(2,128)S(1)}, u32[]{:S(2)}, u32[]{:S(2)}) async-start(f32[64,2,768]{2,1,0:T(2,128)} %reshape.110), calls=%async_computation.2 | async-start | bytes 786432 | tf_op jit(solution)/shard_map/all_to_all | solution.py:285
  50.2 3.2 %collective-permute-start = (f32[4,896]{1,0:T(4,128)S(1)}, f32[4,896]{1,0:T(4,128)S(1)}, u32[]{:S(2)}, u32[]{:S(2)}) collective-permute-start(f32[4,896]{1,0:T(4,128)S(1)} %get-tuple-element.17), channel_id=1, source_target_pairs={{0,128},{128,256},{256,384},{384,0},{1,129},{129,257},{257,385},{3... | collective-permute-start | bytes 43016 | tf_op jit(solution)/shard_map/ppermute | solution.py:228
  53.4 3.3 %collective-permute-start.2 = (f32[4,896]{1,0:T(4,128)S(1)}, f32[4,896]{1,0:T(4,128)S(1)}, u32[]{:S(2)}, u32[]{:S(2)}) collective-permute-start(f32[4,896]{1,0:T(4,128)S(1)} %get-tuple-element.18), channel_id=1, source_target_pairs={{0,384},{128,0},{256,128},{384,256},{1,385},{129,1},{257,129},{385... | collective-permute-start | bytes 43016 | tf_op jit(solution)/shard_map/ppermute | solution.py:228
  56.7 3.5 %collective-permute-start.1 = (f32[4,896]{1,0:T(4,128)S(1)}, f32[4,896]{1,0:T(4,128)S(1)}, u32[]{:S(2)}, u32[]{:S(2)}) collective-permute-start(f32[4,896]{1,0:T(4,128)S(1)} %get-tuple-element.19), channel_id=1, source_target_pairs={{0,256},{128,384},{256,0},{384,128},{1,257},{129,385},{257,1},{385... | collective-permute-start | bytes 43016 | tf_op jit(solution)/shard_map/ppermute | solution.py:228
  60.2 0.0 copy-done.3
  60.2 0.1 slice_reduce_fusion
  60.3 0.0 collective-permute-done
  60.3 0.0 collective-permute-done.2
  60.4 2.6 %collective-permute-done.1 = f32[4,896]{1,0:T(4,128)S(1)} collective-permute-done((f32[4,896]{1,0:T(4,128)S(1)}, f32[4,896]{1,0:T(4,128)S(1)}, u32[]{:S(2)}, u32[]{:S(2)}) %collective-permute-start.1) | collective-permute-done | bytes 14368 | tf_op jit(solution)/shard_map/ppermute | solution.py:228
  62.9 0.0 copy-start
  63.0 5.3 %collective-permute-start.3 = (f32[2,896]{1,0:T(2,128)S(1)}, f32[2,896]{1,0:T(2,128)S(1)}, u32[]{:S(2)}, u32[]{:S(2)}) collective-permute-start(f32[2,896]{1,0:T(2,128)S(1)} %slice.96), channel_id=1, source_target_pairs={{0,32},{32,0},{1,33},{33,1},{2,34},{34,2},{3,35},{35,3},{4,36},{36... | collective-permute-start | bytes 21512 | tf_op jit(solution)/shard_map/ppermute | solution.py:224
  68.2 0.0 all-to-all-done.2
  68.2 0.2 reduce_sum.27
  68.4 0.0 copy-done.1
  68.4 0.1 multiply_reduce_fusion
  68.5 0.7 subtract_multiply_fusion
  69.2 0.0 collective-permute-done.3.moved_ref
  69.2 0.0 copy-done
  69.2 0.0 copy-start.2
  69.2 0.6 copy-done.2
  69.8 1.5 %finish_text.1 = (f32[2,768]{1,0:T(2,128)}, f32[3]{0:T(128)}) custom-call(f32[4,896]{1,0:T(4,128)} %copy-done, f32[2,896]{1,0:T(2,128)} %copy-done.2, bf16[2,768]{1,0:T(2,128)(2,1)} %text_ref.3, f32[1]{0:T(128)} %copy.14.scale_ref), custom_call_target="tpu_custom_call" | custom-call | tf_op jit(solution)/shard_map/finish_text/pallas_call | solution.py:211
  (10 shorter events, 0.1 us)
Async XLA Ops:
  2.0 16.1 %all-to-all-start.1 = ((bf16[8,2,768]{2,1,0:T(2,128)(2,1)}), bf16[8,2,768]{2,1,0:T(2,128)(2,1)S(1)}, u32[]{:S(2)}, u32[]{:S(2)}) async-start(bf16[8,2,768]{2,1,0:T(2,128)(2,1)} %text_blocks.1), calls=%async_computation.1 | async-start | bytes 49152 | tf_op jit(solution)/shard_map/all_to_all | solution.py:255
  18.1 25.1 %all-to-all-start = ((bf16[64,2,896]{2,1,0:T(2,128)(2,1)}), bf16[64,2,896]{2,1,0:T(2,128)(2,1)S(1)}, u32[]{:S(2)}, u32[]{:S(2)}) async-start(bf16[64,2,896]{2,1,0:T(2,128)(2,1)} %get-tuple-element.10), calls=%async_computation | async-start | bytes 458752 | tf_op jit(solution)/shard_map/all_to_all | solution.py:261
  43.3 16.9 %copy-start.3 = (f32[2,128]{1,0:T(2,128)S(1)}, f32[2,128]{1,0:T(2,128)}, u32[]{:S(2)}) copy-start(f32[2,128]{1,0:T(2,128)} %get-tuple-element.12) | copy-start | bytes 3076
  43.6 24.8 %copy-start.1 = (f32[2,768]{1,0:T(2,128)S(1)}, f32[2,768]{1,0:T(2,128)}, u32[]{:S(2)}) copy-start(f32[2,768]{1,0:T(2,128)} %get-tuple-element.11) | copy-start | bytes 18436
  45.2 23.0 %all-to-all-start.2 = ((f32[64,2,768]{2,1,0:T(2,128)}), f32[64,2,768]{2,1,0:T(2,128)S(1)}, u32[]{:S(2)}, u32[]{:S(2)}) async-start(f32[64,2,768]{2,1,0:T(2,128)} %reshape.110), calls=%async_computation.2 | async-start | bytes 786432 | tf_op jit(solution)/shard_map/all_to_all | solution.py:285
  50.2 10.2 %collective-permute-start = (f32[4,896]{1,0:T(4,128)S(1)}, f32[4,896]{1,0:T(4,128)S(1)}, u32[]{:S(2)}, u32[]{:S(2)}) collective-permute-start(f32[4,896]{1,0:T(4,128)S(1)} %get-tuple-element.17), channel_id=1, source_target_pairs={{0,128},{128,256},{256,384},{384,0},{1,129},{129,257},{257,385},{3... | collective-permute-start | bytes 43016 | tf_op jit(solution)/shard_map/ppermute | solution.py:228
  53.4 6.9 %collective-permute-start.2 = (f32[4,896]{1,0:T(4,128)S(1)}, f32[4,896]{1,0:T(4,128)S(1)}, u32[]{:S(2)}, u32[]{:S(2)}) collective-permute-start(f32[4,896]{1,0:T(4,128)S(1)} %get-tuple-element.18), channel_id=1, source_target_pairs={{0,384},{128,0},{256,128},{384,256},{1,385},{129,1},{257,129},{385... | collective-permute-start | bytes 43016 | tf_op jit(solution)/shard_map/ppermute | solution.py:228
  56.7 6.3 %collective-permute-start.1 = (f32[4,896]{1,0:T(4,128)S(1)}, f32[4,896]{1,0:T(4,128)S(1)}, u32[]{:S(2)}, u32[]{:S(2)}) collective-permute-start(f32[4,896]{1,0:T(4,128)S(1)} %get-tuple-element.19), channel_id=1, source_target_pairs={{0,256},{128,384},{256,0},{384,128},{1,257},{129,385},{257,1},{385... | collective-permute-start | bytes 43016 | tf_op jit(solution)/shard_map/ppermute | solution.py:228
  62.9 6.2 %copy-start = (f32[4,896]{1,0:T(4,128)}, f32[4,896]{1,0:T(4,128)S(1)}, u32[]{:S(2)}) copy-start(f32[4,896]{1,0:T(4,128)S(1)} %fusion.11.chip_ref) | copy-start | bytes 43012
  63.0 6.2 %collective-permute-start.3 = (f32[2,896]{1,0:T(2,128)S(1)}, f32[2,896]{1,0:T(2,128)S(1)}, u32[]{:S(2)}, u32[]{:S(2)}) collective-permute-start(f32[2,896]{1,0:T(2,128)S(1)} %slice.96), channel_id=1, source_target_pairs={{0,32},{32,0},{1,33},{33,1},{2,34},{34,2},{3,35},{35,3},{4,36},{36... | collective-permute-start | bytes 21512 | tf_op jit(solution)/shard_map/ppermute | solution.py:224
  69.2 0.6 copy-start.2

commit v5 on v4

--- a/solution.py
+++ b/solution.py
@@ -14,6 +14,7 @@
 BITS = 28
 SIDE = 128
 CHUNK = 256
+PROJ_COPIES = 4
 
 ROW_AXES = ("x", "y_lo", "core")
 BLK_AXES = ("z", "y_hi")
@@ -69,10 +70,19 @@
 ):
     fetch_latent = pltpu.make_async_copy(latent_hbm, latent_ref, sems.at[0])
     fetch_post = pltpu.make_async_copy(post_hbm, post_ref, sems.at[1])
-    fetch_proj = pltpu.make_async_copy(proj_hbm, proj_ref, sems.at[2])
+    depth = proj_hbm.shape[0] // PROJ_COPIES
+    fetch_proj = [
+        pltpu.make_async_copy(
+            proj_hbm.at[pl.ds(part * depth, depth)],
+            proj_ref.at[pl.ds(part * depth, depth)],
+            sems.at[2 + part],
+        )
+        for part in range(PROJ_COPIES)
+    ]
     fetch_latent.start()
     fetch_post.start()
-    fetch_proj.start()
+    for fetch in fetch_proj:
+        fetch.start()
     fetch_latent.wait()
     latent = latent_ref[...]
     bit_count, token_count = latent.shape
@@ -109,13 +119,14 @@
     codes = jnp.transpose(codes, (1, 0)).astype(jnp.bfloat16)
     fetch_post.wait()
     post = post_ref[...]
-    fetch_proj.wait()
-    proj = proj_ref[...]
     sums = []
     for first in range(0, token_count, CHUNK):
         pre_act = jnp.dot(codes[first : first + CHUNK], post, preferred_element_type=jnp.float32)
         hidden = gelu(pre_act).astype(jnp.bfloat16)
-        projected = jnp.dot(hidden, proj, preferred_element_type=jnp.float32)
+        if first == 0:
+            for fetch in fetch_proj:
+                fetch.wait()
+        projected = jnp.dot(hidden, proj_ref[...], preferred_element_type=jnp.float32)
         square = jnp.sum(projected * projected, axis=-1, keepdims=True)
         scaled = projected * lax.rsqrt(square * (1.0 / feat_width) + EPS)
         sums.append(jnp.sum(scaled, axis=0, keepdims=True))
@@ -151,7 +162,7 @@
             pltpu.VMEM(latent.shape, latent.dtype),
             pltpu.VMEM(w_post.shape, w_post.dtype),
             pltpu.VMEM(w_proj.shape, w_proj.dtype),
-            pltpu.SemaphoreType.DMA((3,)),
+            pltpu.SemaphoreType.DMA((2 + PROJ_COPIES,)),
         ],
         compiler_params=pltpu.CompilerParams(vmem_limit_bytes=56 * 1024 * 1024),
         cost_estimate=pl.CostEstimate(
@@ -170,30 +181,38 @@
     return (direction - unit * jnp.sum(unit * direction, axis=-1, keepdims=True)) * inverse
 
 
-def text_kernel(text_ref, block_ref):
-    unit, _ = unit_rows(text_ref[...].astype(jnp.float32))
+def text_kernel(text_ref, block_ref, unit_ref, inv_ref):
+    unit, inverse = unit_rows(text_ref[...].astype(jnp.float32))
+    unit_ref[...] = unit
+    inv_ref[...] = jnp.broadcast_to(inverse, inv_ref.shape)
     unit = unit.astype(jnp.bfloat16)
     for member in range(block_ref.shape[0]):
         block_ref[member] = unit
 
 
 def text_blocks(text_embed, copies):
+    rows = text_embed.shape[0]
     vmem = pl.BlockSpec(memory_space=pltpu.VMEM)
     return pl.pallas_call(
         text_kernel,
-        out_shape=jax.ShapeDtypeStruct((copies,) + text_embed.shape, jnp.bfloat16),
+        out_shape=(
+            jax.ShapeDtypeStruct((copies,) + text_embed.shape, jnp.bfloat16),
+            jax.ShapeDtypeStruct(text_embed.shape, jnp.float32),
+            jax.ShapeDtypeStruct((rows, 128), jnp.float32),
+        ),
         in_specs=[vmem],
-        out_specs=vmem,
+        out_specs=(vmem, vmem, vmem),
         name="text_blocks",
     )(text_embed)
 
 
-def finish_kernel(total_tokens, chip_ref, moved_ref, text_ref, scale_ref, grad_ref, scalar_ref):
-    pair_count, feat_width = text_ref.shape
+def finish_kernel(
+    total_tokens, chip_ref, moved_ref, unit_ref, inv_ref, scale_ref, grad_ref, scalar_ref
+):
+    pair_count, feat_width = unit_ref.shape
     total = chip_ref[:pair_count] + moved_ref[...]
     direction = scale_ref[0] * total[:, :feat_width]
-    unit, inverse = unit_rows(text_ref[...].astype(jnp.float32))
-    grad_ref[...] = tangent(direction, unit, inverse)
+    grad_ref[...] = tangent(direction, unit_ref[...], inv_ref[...][:, :1])
     side = total[:1, feat_width:]
     means = side[:, :32] + side[:, 32:64] + side[:, 64:96]
     means = means * (1.0 / total_tokens)
@@ -205,19 +224,19 @@
     scalar_ref[2] = jnp.sum(jnp.where(place < BITS, spread, 0.0))
 
 
-def finish_text(chip_part, moved, text_embed, logit_scale, total_tokens):
+def finish_text(chip_part, moved, text_unit, text_inv, logit_scale, total_tokens):
     vmem = pl.BlockSpec(memory_space=pltpu.VMEM)
     smem = pl.BlockSpec(memory_space=pltpu.SMEM)
     return pl.pallas_call(
         functools.partial(finish_kernel, total_tokens),
         out_shape=(
-            jax.ShapeDtypeStruct(text_embed.shape, jnp.float32),
+            jax.ShapeDtypeStruct(text_unit.shape, jnp.float32),
             jax.ShapeDtypeStruct((3,), jnp.float32),
         ),
-        in_specs=[vmem, vmem, vmem, smem],
+        in_specs=[vmem, vmem, vmem, vmem, smem],
         out_specs=(vmem, smem),
         name="finish_text",
-    )(chip_part, moved, text_embed, logit_scale)
+    )(chip_part, moved, text_unit, text_inv, logit_scale)
 
 
 def swap_cores(block):
@@ -252,7 +271,8 @@
     scale_value = logit_scale[0]
     bias_value = logit_bias[0]
 
-    group_text = lax.all_to_all(text_blocks(text_embed, n_text), TEXT_AXES, 0, 0)
+    text_block, text_unit, text_inv = text_blocks(text_embed, n_text)
+    group_text = lax.all_to_all(text_block, TEXT_AXES, 0, 0)
     group_text = jnp.concatenate(from_here(group_text, n_x), axis=0)
 
     image_block, image_unit, image_inv = embed_images(
@@ -297,7 +317,9 @@
     image_dir = scale_value * jnp.sum(image_part, axis=0)
     grad_image = tangent(image_dir, image_unit, image_inv[:, :1])
     grad_image, moved = lax.optimization_barrier((grad_image, moved))
-    grad_text, scalars = finish_text(chip_part, moved, text_embed, logit_scale, total_tokens)
+    grad_text, scalars = finish_text(
+        chip_part, moved, text_unit, text_inv, logit_scale, total_tokens
+    )
     return (grad_image, grad_text, scalars)
 
 

time: 71.9 us -> 71.8 us (level)
  no operation moved by 1% of the time
where the time goes in v5:
time: 71.8 us; the launch traced here: 71.2 us
  starting transfers between devices  42.2 us (59%)
  waiting for transfers between devices  14.2 us (20%)
  Pallas kernels  8.81 us (12%)
  between operations  2.2 us (3%)
  local copies, waits for them, and re-layouts  1.99 us (3%)
  other arithmetic  1.15 us (2%)
    all_to_all x1, starting transfers between devices, body(): group_block = lax.all_to_all(image_block, IMAGE_AXES, 0, 0)  12 us
    all_to_all x1, waiting for transfers between devices, body(): group_block = lax.all_to_all(image_block, IMAGE_AXES, 0, 0)  11.6 us
    all_to_all x1, starting transfers between devices, body(): group_text = lax.all_to_all(text_block, TEXT_AXES, 0, 0)  10.1 us
    ppermute x3, starting transfers between devices, along_x(): lax.ppermute(block, 'x', [(i, (i + distance) % count) for i in range(coun...  10 us
    pallas_call x1, Pallas kernels, embed_images(): pl.pallas_call(functools.partial(image_kernel, copies), out_shape=(jax.Sh...  5.91 us
    ppermute x1, starting transfers between devices, swap_cores(): return lax.ppermute(block, 'core', [(0, 1), (1, 0)])  5.24 us
    all_to_all x1, starting transfers between devices, body(): image_part = lax.all_to_all(image_part, IMAGE_AXES, 0, 0)  4.87 us
    ppermute x3, waiting for transfers between devices, along_x(): lax.ppermute(block, 'x', [(i, (i + distance) % count) for i in range(coun...  2.6 us
  transfers between devices with their start and end apart: 7, of which 2 were waited for; matrix products, arithmetic and copies ran while one was open for 2% of the time, Pallas kernels for 8%

profile of v5, /device:TPU:1, one launch (start us, length us, event | category | flops | bytes accessed | tf_op | source)
XLA Modules:
  0.0 71.2 jit_solution(1698349851091608138)
XLA Ops:
  0.6 1.4 %text_blocks.1 = (bf16[8,2,768]{2,1,0:T(2,128)(2,1)}, f32[2,768]{1,0:T(2,128)}, f32[2,128]{1,0:T(2,128)}) custom-call(bf16[2,768]{1,0:T(2,128)(2,1)} %text_ref.1), custom_call_target="tpu_custom_call" | custom-call | tf_op jit(solution)/shard_map/text_blocks/pallas_call | solution.py:196
  2.0 10.1 %all-to-all-start.1 = ((bf16[8,2,768]{2,1,0:T(2,128)(2,1)}), bf16[8,2,768]{2,1,0:T(2,128)(2,1)S(1)}, u32[]{:S(2)}, u32[]{:S(2)}) async-start(bf16[8,2,768]{2,1,0:T(2,128)(2,1)} %get-tuple-element.14), calls=%async_computation.1 | async-start | bytes 49152 | tf_op jit(solution)/shard_map/all_to_all | solution.py:275
  12.1 5.9 %embed_images.1 = (bf16[64,2,896]{2,1,0:T(2,128)(2,1)}, f32[2,768]{1,0:T(2,128)}, f32[2,128]{1,0:T(2,128)}) custom-call(f32[28,1024]{1,0:T(8,128)} %latent_hbm.1, bf16[28,1024]{1,0:T(8,128)(2,1)} %post_hbm.1, bf16[1024,768]{1,0:T(8,128)(2,1)} %proj_hbm.1, f32[768]{0:T(1024)} %gain_ref.1, s32[2]{0:T(128)} %label_ref.1), custom_call_target="tpu_custom_call" | custom-call | flops 2200000000 | bytes 1800000 | tf_op jit(solution)/shard_map/embed_images/pallas_call | solution.py:152
  18.1 0.0 all-to-all-done.1
  18.1 12.0 %all-to-all-start = ((bf16[64,2,896]{2,1,0:T(2,128)(2,1)}), bf16[64,2,896]{2,1,0:T(2,128)(2,1)S(1)}, u32[]{:S(2)}, u32[]{:S(2)}) async-start(bf16[64,2,896]{2,1,0:T(2,128)(2,1)} %get-tuple-element.13), calls=%async_computation | async-start | bytes 458752 | tf_op jit(solution)/shard_map/all_to_all | solution.py:281
  31.5 0.1 concatenate.6
  31.6 11.6 %all-to-all-done = bf16[64,2,896]{2,1,0:T(2,128)(2,1)S(1)} async-done(((bf16[64,2,896]{2,1,0:T(2,128)(2,1)}), bf16[64,2,896]{2,1,0:T(2,128)(2,1)S(1)}, u32[]{:S(2)}, u32[]{:S(2)}) %all-to-all-start) | async-done | bytes 229408 | tf_op jit(solution)/shard_map/all_to_all | solution.py:281
  43.2 0.1 reshape.108
  43.3 0.0 copy-start.3
  43.3 0.1 copy.13
  43.4 0.1 convert_reduce_fusion
  43.6 0.0 copy-start.1
  43.6 0.2 fusion.6
  43.8 0.1 fusion.7
  43.9 0.2 fusion.34
  44.2 1.0 %reshape.110 = f32[64,2,768]{2,1,0:T(2,128)} reshape(f32[128,768]{1,0:T(8,128)S(1)} %fusion.34) | data formatting | bytes 786432 | tf_op jit(solution)/shard_map/reshape | solution.py:304
  45.2 4.9 %all-to-all-start.2 = ((f32[64,2,768]{2,1,0:T(2,128)}), f32[64,2,768]{2,1,0:T(2,128)S(1)}, u32[]{:S(2)}, u32[]{:S(2)}) async-start(f32[64,2,768]{2,1,0:T(2,128)} %reshape.110), calls=%async_computation.2 | async-start | bytes 786432 | tf_op jit(solution)/shard_map/all_to_all | solution.py:305
  50.1 3.2 %collective-permute-start = (f32[4,896]{1,0:T(4,128)S(1)}, f32[4,896]{1,0:T(4,128)S(1)}, u32[]{:S(2)}, u32[]{:S(2)}) collective-permute-start(f32[4,896]{1,0:T(4,128)S(1)} %get-tuple-element.23), channel_id=1, source_target_pairs={{0,128},{128,256},{256,384},{384,0},{1,129},{129,257},{257,385},{3... | collective-permute-start | bytes 43016 | tf_op jit(solution)/shard_map/ppermute | solution.py:247
  53.3 3.3 %collective-permute-start.2 = (f32[4,896]{1,0:T(4,128)S(1)}, f32[4,896]{1,0:T(4,128)S(1)}, u32[]{:S(2)}, u32[]{:S(2)}) collective-permute-start(f32[4,896]{1,0:T(4,128)S(1)} %get-tuple-element.24), channel_id=1, source_target_pairs={{0,384},{128,0},{256,128},{384,256},{1,385},{129,1},{257,129},{385... | collective-permute-start | bytes 43016 | tf_op jit(solution)/shard_map/ppermute | solution.py:247
  56.6 3.5 %collective-permute-start.1 = (f32[4,896]{1,0:T(4,128)S(1)}, f32[4,896]{1,0:T(4,128)S(1)}, u32[]{:S(2)}, u32[]{:S(2)}) collective-permute-start(f32[4,896]{1,0:T(4,128)S(1)} %get-tuple-element.25), channel_id=1, source_target_pairs={{0,256},{128,384},{256,0},{384,128},{1,257},{129,385},{257,1},{385... | collective-permute-start | bytes 43016 | tf_op jit(solution)/shard_map/ppermute | solution.py:247
  60.1 0.0 copy-done.3
  60.1 0.1 slice_reduce_fusion
  60.2 0.0 collective-permute-done
  60.2 0.0 collective-permute-done.2
  60.3 2.6 %collective-permute-done.1 = f32[4,896]{1,0:T(4,128)S(1)} collective-permute-done((f32[4,896]{1,0:T(4,128)S(1)}, f32[4,896]{1,0:T(4,128)S(1)}, u32[]{:S(2)}, u32[]{:S(2)}) %collective-permute-start.1) | collective-permute-done | bytes 14368 | tf_op jit(solution)/shard_map/ppermute | solution.py:247
  62.9 0.0 copy-start
  62.9 5.2 %collective-permute-start.3 = (f32[2,896]{1,0:T(2,128)S(1)}, f32[2,896]{1,0:T(2,128)S(1)}, u32[]{:S(2)}, u32[]{:S(2)}) collective-permute-start(f32[2,896]{1,0:T(2,128)S(1)} %slice.96), channel_id=1, source_target_pairs={{0,32},{32,0},{1,33},{33,1},{2,34},{34,2},{3,35},{35,3},{4,36},{36... | collective-permute-start | bytes 21512 | tf_op jit(solution)/shard_map/ppermute | solution.py:243
  68.1 0.0 all-to-all-done.2
  68.2 0.2 reduce_sum.27
  68.3 0.0 copy-done.1
  68.3 0.1 multiply_reduce_fusion
  68.4 0.7 subtract_multiply_fusion
  69.1 0.0 collective-permute-done.3.moved_ref
  69.1 0.0 copy-start.2
  69.1 0.0 copy-done
  69.1 0.6 copy-done.2
  69.7 1.5 %finish_text.1 = (f32[2,768]{1,0:T(2,128)}, f32[3]{0:T(128)}) custom-call(f32[4,896]{1,0:T(4,128)} %copy-done, f32[2,896]{1,0:T(2,128)} %copy-done.2, f32[2,768]{1,0:T(2,128)} %get-tuple-element.19.unit_ref, f32[2,128]{1,0:T(2,128)} %get-tuple-element.20.inv_ref, f32[1]{0:T(128)} %copy.14.scale_ref), custom_call_target="tpu_custom_call" | custom-call | tf_op jit(solution)/shard_map/finish_text/pallas_call | solution.py:230
  (10 shorter events, 0.1 us)
Async XLA Ops:
  2.0 16.0 %all-to-all-start.1 = ((bf16[8,2,768]{2,1,0:T(2,128)(2,1)}), bf16[8,2,768]{2,1,0:T(2,128)(2,1)S(1)}, u32[]{:S(2)}, u32[]{:S(2)}) async-start(bf16[8,2,768]{2,1,0:T(2,128)(2,1)} %get-tuple-element.14), calls=%async_computation.1 | async-start | bytes 49152 | tf_op jit(solution)/shard_map/all_to_all | solution.py:275
  18.1 25.1 %all-to-all-start = ((bf16[64,2,896]{2,1,0:T(2,128)(2,1)}), bf16[64,2,896]{2,1,0:T(2,128)(2,1)S(1)}, u32[]{:S(2)}, u32[]{:S(2)}) async-start(bf16[64,2,896]{2,1,0:T(2,128)(2,1)} %get-tuple-element.13), calls=%async_computation | async-start | bytes 458752 | tf_op jit(solution)/shard_map/all_to_all | solution.py:281
  43.3 16.8 %copy-start.3 = (f32[2,128]{1,0:T(2,128)S(1)}, f32[2,128]{1,0:T(2,128)}, u32[]{:S(2)}) copy-start(f32[2,128]{1,0:T(2,128)} %get-tuple-element.16) | copy-start | bytes 3076
  43.6 24.7 %copy-start.1 = (f32[2,768]{1,0:T(2,128)S(1)}, f32[2,768]{1,0:T(2,128)}, u32[]{:S(2)}) copy-start(f32[2,768]{1,0:T(2,128)} %get-tuple-element.15) | copy-start | bytes 18436
  45.2 23.0 %all-to-all-start.2 = ((f32[64,2,768]{2,1,0:T(2,128)}), f32[64,2,768]{2,1,0:T(2,128)S(1)}, u32[]{:S(2)}, u32[]{:S(2)}) async-start(f32[64,2,768]{2,1,0:T(2,128)} %reshape.110), calls=%async_computation.2 | async-start | bytes 786432 | tf_op jit(solution)/shard_map/all_to_all | solution.py:305
  50.1 10.2 %collective-permute-start = (f32[4,896]{1,0:T(4,128)S(1)}, f32[4,896]{1,0:T(4,128)S(1)}, u32[]{:S(2)}, u32[]{:S(2)}) collective-permute-start(f32[4,896]{1,0:T(4,128)S(1)} %get-tuple-element.23), channel_id=1, source_target_pairs={{0,128},{128,256},{256,384},{384,0},{1,129},{129,257},{257,385},{3... | collective-permute-start | bytes 43016 | tf_op jit(solution)/shard_map/ppermute | solution.py:247
  53.3 6.9 %collective-permute-start.2 = (f32[4,896]{1,0:T(4,128)S(1)}, f32[4,896]{1,0:T(4,128)S(1)}, u32[]{:S(2)}, u32[]{:S(2)}) collective-permute-start(f32[4,896]{1,0:T(4,128)S(1)} %get-tuple-element.24), channel_id=1, source_target_pairs={{0,384},{128,0},{256,128},{384,256},{1,385},{129,1},{257,129},{385... | collective-permute-start | bytes 43016 | tf_op jit(solution)/shard_map/ppermute | solution.py:247
  56.6 6.3 %collective-permute-start.1 = (f32[4,896]{1,0:T(4,128)S(1)}, f32[4,896]{1,0:T(4,128)S(1)}, u32[]{:S(2)}, u32[]{:S(2)}) collective-permute-start(f32[4,896]{1,0:T(4,128)S(1)} %get-tuple-element.25), channel_id=1, source_target_pairs={{0,256},{128,384},{256,0},{384,128},{1,257},{129,385},{257,1},{385... | collective-permute-start | bytes 43016 | tf_op jit(solution)/shard_map/ppermute | solution.py:247
  62.9 6.2 %copy-start = (f32[4,896]{1,0:T(4,128)}, f32[4,896]{1,0:T(4,128)S(1)}, u32[]{:S(2)}) copy-start(f32[4,896]{1,0:T(4,128)S(1)} %fusion.11.chip_ref) | copy-start | bytes 43012
  62.9 6.2 %collective-permute-start.3 = (f32[2,896]{1,0:T(2,128)S(1)}, f32[2,896]{1,0:T(2,128)S(1)}, u32[]{:S(2)}, u32[]{:S(2)}) collective-permute-start(f32[2,896]{1,0:T(2,128)S(1)} %slice.96), channel_id=1, source_target_pairs={{0,32},{32,0},{1,33},{33,1},{2,34},{34,2},{3,35},{35,3},{4,36},{36... | collective-permute-start | bytes 21512 | tf_op jit(solution)/shard_map/ppermute | solution.py:243
  69.1 0.6 copy-start.2

commit v6 on v5

--- a/solution.py
+++ b/solution.py
@@ -207,10 +207,26 @@
 
 
 def finish_kernel(
-    total_tokens, chip_ref, moved_ref, unit_ref, inv_ref, scale_ref, grad_ref, scalar_ref
+    total_tokens,
+    chip_any,
+    moved_any,
+    unit_ref,
+    inv_ref,
+    scale_ref,
+    grad_ref,
+    scalar_ref,
+    chip_ref,
+    moved_ref,
+    sems,
 ):
     pair_count, feat_width = unit_ref.shape
-    total = chip_ref[:pair_count] + moved_ref[...]
+    fetch_chip = pltpu.make_async_copy(chip_any, chip_ref, sems.at[0])
+    fetch_moved = pltpu.make_async_copy(moved_any, moved_ref, sems.at[1])
+    fetch_chip.start()
+    fetch_moved.start()
+    fetch_chip.wait()
+    fetch_moved.wait()
+    total = chip_ref[...][:pair_count] + moved_ref[...]
     direction = scale_ref[0] * total[:, :feat_width]
     grad_ref[...] = tangent(direction, unit_ref[...], inv_ref[...][:, :1])
     side = total[:1, feat_width:]
@@ -227,14 +243,20 @@
 def finish_text(chip_part, moved, text_unit, text_inv, logit_scale, total_tokens):
     vmem = pl.BlockSpec(memory_space=pltpu.VMEM)
     smem = pl.BlockSpec(memory_space=pltpu.SMEM)
+    where = pl.BlockSpec(memory_space=pl.ANY)
     return pl.pallas_call(
         functools.partial(finish_kernel, total_tokens),
         out_shape=(
             jax.ShapeDtypeStruct(text_unit.shape, jnp.float32),
             jax.ShapeDtypeStruct((3,), jnp.float32),
         ),
-        in_specs=[vmem, vmem, vmem, vmem, smem],
+        in_specs=[where, where, vmem, vmem, smem],
         out_specs=(vmem, smem),
+        scratch_shapes=[
+            pltpu.VMEM(chip_part.shape, chip_part.dtype),
+            pltpu.VMEM(moved.shape, moved.dtype),
+            pltpu.SemaphoreType.DMA((2,)),
+        ],
         name="finish_text",
     )(chip_part, moved, text_unit, text_inv, logit_scale)
 

time: 71.8 us -> 72.5 us (level)
  no operation moved by 1% of the time
where the time goes in v6:
time: 72.5 us; the launch traced here: 71.9 us
  starting transfers between devices  42.2 us (58%)
  waiting for transfers between devices  14.2 us (20%)
  Pallas kernels  9.5 us (13%)
  between operations  2.2 us (3%)
  local copies, waits for them, and re-layouts  1.99 us (3%)
  other arithmetic  1.15 us (2%)
    all_to_all x1, starting transfers between devices, body(): group_block = lax.all_to_all(image_block, IMAGE_AXES, 0, 0)  12 us
    all_to_all x1, waiting for transfers between devices, body(): group_block = lax.all_to_all(image_block, IMAGE_AXES, 0, 0)  11.6 us
    all_to_all x1, starting transfers between devices, body(): group_text = lax.all_to_all(text_block, TEXT_AXES, 0, 0)  10.1 us
    ppermute x3, starting transfers between devices, along_x(): lax.ppermute(block, 'x', [(i, (i + distance) % count) for i in range(coun...  10 us
    pallas_call x1, Pallas kernels, embed_images(): pl.pallas_call(functools.partial(image_kernel, copies), out_shape=(jax.Sh...  5.91 us
    ppermute x1, starting transfers between devices, swap_cores(): return lax.ppermute(block, 'core', [(0, 1), (1, 0)])  5.24 us
    all_to_all x1, starting transfers between devices, body(): image_part = lax.all_to_all(image_part, IMAGE_AXES, 0, 0)  4.87 us
    ppermute x3, waiting for transfers between devices, along_x(): lax.ppermute(block, 'x', [(i, (i + distance) % count) for i in range(coun...  2.6 us
  transfers between devices with their start and end apart: 7, of which 2 were waited for; matrix products, arithmetic and copies ran while one was open for 2% of the time, Pallas kernels for 8%

profile of v6, /device:TPU:1, one launch (start us, length us, event | category | flops | bytes accessed | tf_op | source)
XLA Modules:
  0.0 71.9 jit_solution(10670954613291820898)
XLA Ops:
  0.6 1.4 %text_blocks.1 = (bf16[8,2,768]{2,1,0:T(2,128)(2,1)}, f32[2,768]{1,0:T(2,128)}, f32[2,128]{1,0:T(2,128)}) custom-call(bf16[2,768]{1,0:T(2,128)(2,1)} %text_ref.1), custom_call_target="tpu_custom_call" | custom-call | tf_op jit(solution)/shard_map/text_blocks/pallas_call | solution.py:196
  2.0 10.1 %all-to-all-start.1 = ((bf16[8,2,768]{2,1,0:T(2,128)(2,1)}), bf16[8,2,768]{2,1,0:T(2,128)(2,1)S(1)}, u32[]{:S(2)}, u32[]{:S(2)}) async-start(bf16[8,2,768]{2,1,0:T(2,128)(2,1)} %get-tuple-element.14), calls=%async_computation.1 | async-start | bytes 49152 | tf_op jit(solution)/shard_map/all_to_all | solution.py:297
  12.1 5.9 %embed_images.1 = (bf16[64,2,896]{2,1,0:T(2,128)(2,1)}, f32[2,768]{1,0:T(2,128)}, f32[2,128]{1,0:T(2,128)}) custom-call(f32[28,1024]{1,0:T(8,128)} %latent_hbm.1, bf16[28,1024]{1,0:T(8,128)(2,1)} %post_hbm.1, bf16[1024,768]{1,0:T(8,128)(2,1)} %proj_hbm.1, f32[768]{0:T(1024)} %gain_ref.1, s32[2]{0:T(128)} %label_ref.1), custom_call_target="tpu_custom_call" | custom-call | flops 2200000000 | bytes 1800000 | tf_op jit(solution)/shard_map/embed_images/pallas_call | solution.py:152
  18.1 0.0 all-to-all-done.1
  18.1 12.0 %all-to-all-start = ((bf16[64,2,896]{2,1,0:T(2,128)(2,1)}), bf16[64,2,896]{2,1,0:T(2,128)(2,1)S(1)}, u32[]{:S(2)}, u32[]{:S(2)}) async-start(bf16[64,2,896]{2,1,0:T(2,128)(2,1)} %get-tuple-element.13), calls=%async_computation | async-start | bytes 458752 | tf_op jit(solution)/shard_map/all_to_all | solution.py:303
  31.5 0.1 concatenate.6
  31.6 11.6 %all-to-all-done = bf16[64,2,896]{2,1,0:T(2,128)(2,1)S(1)} async-done(((bf16[64,2,896]{2,1,0:T(2,128)(2,1)}), bf16[64,2,896]{2,1,0:T(2,128)(2,1)S(1)}, u32[]{:S(2)}, u32[]{:S(2)}) %all-to-all-start) | async-done | bytes 229408 | tf_op jit(solution)/shard_map/all_to_all | solution.py:303
  43.2 0.1 reshape.108
  43.3 0.0 copy-start.3
  43.3 0.1 copy.13
  43.4 0.1 convert_reduce_fusion
  43.6 0.0 copy-start.1
  43.6 0.2 fusion.6
  43.8 0.1 fusion.7
  43.9 0.2 fusion.34
  44.2 1.0 %reshape.110 = f32[64,2,768]{2,1,0:T(2,128)} reshape(f32[128,768]{1,0:T(8,128)S(1)} %fusion.34) | data formatting | bytes 786432 | tf_op jit(solution)/shard_map/reshape | solution.py:326
  45.2 4.9 %all-to-all-start.2 = ((f32[64,2,768]{2,1,0:T(2,128)}), f32[64,2,768]{2,1,0:T(2,128)S(1)}, u32[]{:S(2)}, u32[]{:S(2)}) async-start(f32[64,2,768]{2,1,0:T(2,128)} %reshape.110), calls=%async_computation.2 | async-start | bytes 786432 | tf_op jit(solution)/shard_map/all_to_all | solution.py:327
  50.1 3.2 %collective-permute-start = (f32[4,896]{1,0:T(4,128)S(1)}, f32[4,896]{1,0:T(4,128)S(1)}, u32[]{:S(2)}, u32[]{:S(2)}) collective-permute-start(f32[4,896]{1,0:T(4,128)S(1)} %get-tuple-element.23), channel_id=1, source_target_pairs={{0,128},{128,256},{256,384},{384,0},{1,129},{129,257},{257,385},{3... | collective-permute-start | bytes 43016 | tf_op jit(solution)/shard_map/ppermute | solution.py:269
  53.3 3.3 %collective-permute-start.2 = (f32[4,896]{1,0:T(4,128)S(1)}, f32[4,896]{1,0:T(4,128)S(1)}, u32[]{:S(2)}, u32[]{:S(2)}) collective-permute-start(f32[4,896]{1,0:T(4,128)S(1)} %get-tuple-element.24), channel_id=1, source_target_pairs={{0,384},{128,0},{256,128},{384,256},{1,385},{129,1},{257,129},{385... | collective-permute-start | bytes 43016 | tf_op jit(solution)/shard_map/ppermute | solution.py:269
  56.6 3.5 %collective-permute-start.1 = (f32[4,896]{1,0:T(4,128)S(1)}, f32[4,896]{1,0:T(4,128)S(1)}, u32[]{:S(2)}, u32[]{:S(2)}) collective-permute-start(f32[4,896]{1,0:T(4,128)S(1)} %get-tuple-element.25), channel_id=1, source_target_pairs={{0,256},{128,384},{256,0},{384,128},{1,257},{129,385},{257,1},{385... | collective-permute-start | bytes 43016 | tf_op jit(solution)/shard_map/ppermute | solution.py:269
  60.1 0.0 copy-done.3
  60.1 0.1 slice_reduce_fusion
  60.2 0.0 collective-permute-done
  60.2 0.0 collective-permute-done.2
  60.3 2.6 %collective-permute-done.1 = f32[4,896]{1,0:T(4,128)S(1)} collective-permute-done((f32[4,896]{1,0:T(4,128)S(1)}, f32[4,896]{1,0:T(4,128)S(1)}, u32[]{:S(2)}, u32[]{:S(2)}) %collective-permute-start.1) | collective-permute-done | bytes 14368 | tf_op jit(solution)/shard_map/ppermute | solution.py:269
  62.9 0.0 copy-start
  62.9 5.2 %collective-permute-start.3 = (f32[2,896]{1,0:T(2,128)S(1)}, f32[2,896]{1,0:T(2,128)S(1)}, u32[]{:S(2)}, u32[]{:S(2)}) collective-permute-start(f32[2,896]{1,0:T(2,128)S(1)} %slice.96), channel_id=1, source_target_pairs={{0,32},{32,0},{1,33},{33,1},{2,34},{34,2},{3,35},{35,3},{4,36},{36... | collective-permute-start | bytes 21512 | tf_op jit(solution)/shard_map/ppermute | solution.py:265
  68.1 0.0 all-to-all-done.2
  68.2 0.2 reduce_sum.27
  68.3 0.0 copy-done.1
  68.3 0.1 multiply_reduce_fusion
  68.4 0.7 subtract_multiply_fusion
  69.1 0.0 collective-permute-done.3.moved_any
  69.1 0.0 copy-start.2
  69.1 0.0 copy-done
  69.1 0.6 copy-done.2
  69.7 2.2 %finish_text.1 = (f32[2,768]{1,0:T(2,128)}, f32[3]{0:T(128)}) custom-call(f32[4,896]{1,0:T(4,128)} %copy-done, f32[2,896]{1,0:T(2,128)} %copy-done.2, f32[2,768]{1,0:T(2,128)} %get-tuple-element.19.unit_ref, f32[2,128]{1,0:T(2,128)} %get-tuple-element.20.inv_ref, f32[1]{0:T(128)} %copy.14.scale_ref), custom_call_target="tpu_custom_call" | custom-call | tf_op jit(solution)/shard_map/finish_text/pallas_call | solution.py:247
  (10 shorter events, 0.1 us)
Async XLA Ops:
  2.0 16.0 %all-to-all-start.1 = ((bf16[8,2,768]{2,1,0:T(2,128)(2,1)}), bf16[8,2,768]{2,1,0:T(2,128)(2,1)S(1)}, u32[]{:S(2)}, u32[]{:S(2)}) async-start(bf16[8,2,768]{2,1,0:T(2,128)(2,1)} %get-tuple-element.14), calls=%async_computation.1 | async-start | bytes 49152 | tf_op jit(solution)/shard_map/all_to_all | solution.py:297
  18.1 25.1 %all-to-all-start = ((bf16[64,2,896]{2,1,0:T(2,128)(2,1)}), bf16[64,2,896]{2,1,0:T(2,128)(2,1)S(1)}, u32[]{:S(2)}, u32[]{:S(2)}) async-start(bf16[64,2,896]{2,1,0:T(2,128)(2,1)} %get-tuple-element.13), calls=%async_computation | async-start | bytes 458752 | tf_op jit(solution)/shard_map/all_to_all | solution.py:303
  43.3 16.8 %copy-start.3 = (f32[2,128]{1,0:T(2,128)S(1)}, f32[2,128]{1,0:T(2,128)}, u32[]{:S(2)}) copy-start(f32[2,128]{1,0:T(2,128)} %get-tuple-element.16) | copy-start | bytes 3076
  43.6 24.7 %copy-start.1 = (f32[2,768]{1,0:T(2,128)S(1)}, f32[2,768]{1,0:T(2,128)}, u32[]{:S(2)}) copy-start(f32[2,768]{1,0:T(2,128)} %get-tuple-element.15) | copy-start | bytes 18436
  45.2 23.0 %all-to-all-start.2 = ((f32[64,2,768]{2,1,0:T(2,128)}), f32[64,2,768]{2,1,0:T(2,128)S(1)}, u32[]{:S(2)}, u32[]{:S(2)}) async-start(f32[64,2,768]{2,1,0:T(2,128)} %reshape.110), calls=%async_computation.2 | async-start | bytes 786432 | tf_op jit(solution)/shard_map/all_to_all | solution.py:327
  50.1 10.2 %collective-permute-start = (f32[4,896]{1,0:T(4,128)S(1)}, f32[4,896]{1,0:T(4,128)S(1)}, u32[]{:S(2)}, u32[]{:S(2)}) collective-permute-start(f32[4,896]{1,0:T(4,128)S(1)} %get-tuple-element.23), channel_id=1, source_target_pairs={{0,128},{128,256},{256,384},{384,0},{1,129},{129,257},{257,385},{3... | collective-permute-start | bytes 43016 | tf_op jit(solution)/shard_map/ppermute | solution.py:269
  53.3 6.9 %collective-permute-start.2 = (f32[4,896]{1,0:T(4,128)S(1)}, f32[4,896]{1,0:T(4,128)S(1)}, u32[]{:S(2)}, u32[]{:S(2)}) collective-permute-start(f32[4,896]{1,0:T(4,128)S(1)} %get-tuple-element.24), channel_id=1, source_target_pairs={{0,384},{128,0},{256,128},{384,256},{1,385},{129,1},{257,129},{385... | collective-permute-start | bytes 43016 | tf_op jit(solution)/shard_map/ppermute | solution.py:269
  56.6 6.3 %collective-permute-start.1 = (f32[4,896]{1,0:T(4,128)S(1)}, f32[4,896]{1,0:T(4,128)S(1)}, u32[]{:S(2)}, u32[]{:S(2)}) collective-permute-start(f32[4,896]{1,0:T(4,128)S(1)} %get-tuple-element.25), channel_id=1, source_target_pairs={{0,256},{128,384},{256,0},{384,128},{1,257},{129,385},{257,1},{385... | collective-permute-start | bytes 43016 | tf_op jit(solution)/shard_map/ppermute | solution.py:269
  62.9 6.2 %copy-start = (f32[4,896]{1,0:T(4,128)}, f32[4,896]{1,0:T(4,128)S(1)}, u32[]{:S(2)}) copy-start(f32[4,896]{1,0:T(4,128)S(1)} %fusion.11.chip_any) | copy-start | bytes 43012
  62.9 6.2 %collective-permute-start.3 = (f32[2,896]{1,0:T(2,128)S(1)}, f32[2,896]{1,0:T(2,128)S(1)}, u32[]{:S(2)}, u32[]{:S(2)}) collective-permute-start(f32[2,896]{1,0:T(2,128)S(1)} %slice.96), channel_id=1, source_target_pairs={{0,32},{32,0},{1,33},{33,1},{2,34},{34,2},{3,35},{35,3},{4,36},{36... | collective-permute-start | bytes 21512 | tf_op jit(solution)/shard_map/ppermute | solution.py:265
  69.1 0.6 copy-start.2

commit v7 on v5

--- a/solution.py
+++ b/solution.py
@@ -13,7 +13,7 @@
 SHARPNESS = 4.0
 BITS = 28
 SIDE = 128
-CHUNK = 256
+CHUNK = 512
 PROJ_COPIES = 4
 
 ROW_AXES = ("x", "y_lo", "core")

time: 71.8 us -> 71.9 us (level)
  no operation moved by 1% of the time
where the time goes in v7:
time: 71.9 us; the launch traced here: 71.3 us
  starting transfers between devices  42.2 us (59%)
  waiting for transfers between devices  14.2 us (20%)
  Pallas kernels  8.94 us (12%)
  between operations  2.2 us (3%)
  local copies, waits for them, and re-layouts  1.99 us (3%)
  other arithmetic  1.15 us (2%)
    all_to_all x1, starting transfers between devices, body(): group_block = lax.all_to_all(image_block, IMAGE_AXES, 0, 0)  12 us
    all_to_all x1, waiting for transfers between devices, body(): group_block = lax.all_to_all(image_block, IMAGE_AXES, 0, 0)  11.6 us
    all_to_all x1, starting transfers between devices, body(): group_text = lax.all_to_all(text_block, TEXT_AXES, 0, 0)  10.1 us
    ppermute x3, starting transfers between devices, along_x(): lax.ppermute(block, 'x', [(i, (i + distance) % count) for i in range(coun...  10 us
    pallas_call x1, Pallas kernels, embed_images(): pl.pallas_call(functools.partial(image_kernel, copies), out_shape=(jax.Sh...  6.04 us
    ppermute x1, starting transfers between devices, swap_cores(): return lax.ppermute(block, 'core', [(0, 1), (1, 0)])  5.24 us
    all_to_all x1, starting transfers between devices, body(): image_part = lax.all_to_all(image_part, IMAGE_AXES, 0, 0)  4.87 us
    ppermute x3, waiting for transfers between devices, along_x(): lax.ppermute(block, 'x', [(i, (i + distance) % count) for i in range(coun...  2.6 us
  transfers between devices with their start and end apart: 7, of which 2 were waited for; matrix products, arithmetic and copies ran while one was open for 2% of the time, Pallas kernels for 8%

profile of v7, /device:TPU:1, one launch (start us, length us, event | category | flops | bytes accessed | tf_op | source)
XLA Modules:
  0.0 71.3 jit_solution(1657437375727996214)
XLA Ops:
  0.6 1.4 %text_blocks.1 = (bf16[8,2,768]{2,1,0:T(2,128)(2,1)}, f32[2,768]{1,0:T(2,128)}, f32[2,128]{1,0:T(2,128)}) custom-call(bf16[2,768]{1,0:T(2,128)(2,1)} %text_ref.1), custom_call_target="tpu_custom_call" | custom-call | tf_op jit(solution)/shard_map/text_blocks/pallas_call | solution.py:196
  2.0 10.1 %all-to-all-start.1 = ((bf16[8,2,768]{2,1,0:T(2,128)(2,1)}), bf16[8,2,768]{2,1,0:T(2,128)(2,1)S(1)}, u32[]{:S(2)}, u32[]{:S(2)}) async-start(bf16[8,2,768]{2,1,0:T(2,128)(2,1)} %get-tuple-element.14), calls=%async_computation.1 | async-start | bytes 49152 | tf_op jit(solution)/shard_map/all_to_all | solution.py:275
  12.1 6.0 %embed_images.1 = (bf16[64,2,896]{2,1,0:T(2,128)(2,1)}, f32[2,768]{1,0:T(2,128)}, f32[2,128]{1,0:T(2,128)}) custom-call(f32[28,1024]{1,0:T(8,128)} %latent_hbm.1, bf16[28,1024]{1,0:T(8,128)(2,1)} %post_hbm.1, bf16[1024,768]{1,0:T(8,128)(2,1)} %proj_hbm.1, f32[768]{0:T(1024)} %gain_ref.1, s32[2]{0:T(128)} %label_ref.1), custom_call_target="tpu_custom_call" | custom-call | flops 2200000000 | bytes 1800000 | tf_op jit(solution)/shard_map/embed_images/pallas_call | solution.py:152
  18.2 0.0 all-to-all-done.1
  18.2 12.0 %all-to-all-start = ((bf16[64,2,896]{2,1,0:T(2,128)(2,1)}), bf16[64,2,896]{2,1,0:T(2,128)(2,1)S(1)}, u32[]{:S(2)}, u32[]{:S(2)}) async-start(bf16[64,2,896]{2,1,0:T(2,128)(2,1)} %get-tuple-element.13), calls=%async_computation | async-start | bytes 458752 | tf_op jit(solution)/shard_map/all_to_all | solution.py:281
  31.6 0.1 concatenate.6
  31.7 11.6 %all-to-all-done = bf16[64,2,896]{2,1,0:T(2,128)(2,1)S(1)} async-done(((bf16[64,2,896]{2,1,0:T(2,128)(2,1)}), bf16[64,2,896]{2,1,0:T(2,128)(2,1)S(1)}, u32[]{:S(2)}, u32[]{:S(2)}) %all-to-all-start) | async-done | bytes 229408 | tf_op jit(solution)/shard_map/all_to_all | solution.py:281
  43.3 0.1 reshape.108
  43.4 0.0 copy-start.3
  43.4 0.1 copy.13
  43.6 0.1 convert_reduce_fusion
  43.7 0.0 copy-start.1
  43.7 0.2 fusion.6
  43.9 0.1 fusion.7
  44.1 0.2 fusion.34
  44.3 1.0 %reshape.110 = f32[64,2,768]{2,1,0:T(2,128)} reshape(f32[128,768]{1,0:T(8,128)S(1)} %fusion.34) | data formatting | bytes 786432 | tf_op jit(solution)/shard_map/reshape | solution.py:304
  45.3 4.9 %all-to-all-start.2 = ((f32[64,2,768]{2,1,0:T(2,128)}), f32[64,2,768]{2,1,0:T(2,128)S(1)}, u32[]{:S(2)}, u32[]{:S(2)}) async-start(f32[64,2,768]{2,1,0:T(2,128)} %reshape.110), calls=%async_computation.2 | async-start | bytes 786432 | tf_op jit(solution)/shard_map/all_to_all | solution.py:305
  50.2 3.2 %collective-permute-start = (f32[4,896]{1,0:T(4,128)S(1)}, f32[4,896]{1,0:T(4,128)S(1)}, u32[]{:S(2)}, u32[]{:S(2)}) collective-permute-start(f32[4,896]{1,0:T(4,128)S(1)} %get-tuple-element.23), channel_id=1, source_target_pairs={{0,128},{128,256},{256,384},{384,0},{1,129},{129,257},{257,385},{3... | collective-permute-start | bytes 43016 | tf_op jit(solution)/shard_map/ppermute | solution.py:247
  53.4 3.3 %collective-permute-start.2 = (f32[4,896]{1,0:T(4,128)S(1)}, f32[4,896]{1,0:T(4,128)S(1)}, u32[]{:S(2)}, u32[]{:S(2)}) collective-permute-start(f32[4,896]{1,0:T(4,128)S(1)} %get-tuple-element.24), channel_id=1, source_target_pairs={{0,384},{128,0},{256,128},{384,256},{1,385},{129,1},{257,129},{385... | collective-permute-start | bytes 43016 | tf_op jit(solution)/shard_map/ppermute | solution.py:247
  56.7 3.5 %collective-permute-start.1 = (f32[4,896]{1,0:T(4,128)S(1)}, f32[4,896]{1,0:T(4,128)S(1)}, u32[]{:S(2)}, u32[]{:S(2)}) collective-permute-start(f32[4,896]{1,0:T(4,128)S(1)} %get-tuple-element.25), channel_id=1, source_target_pairs={{0,256},{128,384},{256,0},{384,128},{1,257},{129,385},{257,1},{385... | collective-permute-start | bytes 43016 | tf_op jit(solution)/shard_map/ppermute | solution.py:247
  60.2 0.0 copy-done.3
  60.3 0.1 slice_reduce_fusion
  60.4 0.0 collective-permute-done
  60.4 0.0 collective-permute-done.2
  60.4 2.6 %collective-permute-done.1 = f32[4,896]{1,0:T(4,128)S(1)} collective-permute-done((f32[4,896]{1,0:T(4,128)S(1)}, f32[4,896]{1,0:T(4,128)S(1)}, u32[]{:S(2)}, u32[]{:S(2)}) %collective-permute-start.1) | collective-permute-done | bytes 14368 | tf_op jit(solution)/shard_map/ppermute | solution.py:247
  63.0 0.0 copy-start
  63.0 5.2 %collective-permute-start.3 = (f32[2,896]{1,0:T(2,128)S(1)}, f32[2,896]{1,0:T(2,128)S(1)}, u32[]{:S(2)}, u32[]{:S(2)}) collective-permute-start(f32[2,896]{1,0:T(2,128)S(1)} %slice.96), channel_id=1, source_target_pairs={{0,32},{32,0},{1,33},{33,1},{2,34},{34,2},{3,35},{35,3},{4,36},{36... | collective-permute-start | bytes 21512 | tf_op jit(solution)/shard_map/ppermute | solution.py:243
  68.3 0.0 all-to-all-done.2
  68.3 0.2 reduce_sum.27
  68.4 0.0 copy-done.1
  68.4 0.1 multiply_reduce_fusion
  68.6 0.7 subtract_multiply_fusion
  69.2 0.0 collective-permute-done.3.moved_ref
  69.2 0.0 copy-start.2
  69.2 0.0 copy-done
  69.2 0.6 copy-done.2
  69.8 1.5 %finish_text.1 = (f32[2,768]{1,0:T(2,128)}, f32[3]{0:T(128)}) custom-call(f32[4,896]{1,0:T(4,128)} %copy-done, f32[2,896]{1,0:T(2,128)} %copy-done.2, f32[2,768]{1,0:T(2,128)} %get-tuple-element.19.unit_ref, f32[2,128]{1,0:T(2,128)} %get-tuple-element.20.inv_ref, f32[1]{0:T(128)} %copy.14.scale_ref), custom_call_target="tpu_custom_call" | custom-call | tf_op jit(solution)/shard_map/finish_text/pallas_call | solution.py:230
  (10 shorter events, 0.1 us)
Async XLA Ops:
  2.0 16.2 %all-to-all-start.1 = ((bf16[8,2,768]{2,1,0:T(2,128)(2,1)}), bf16[8,2,768]{2,1,0:T(2,128)(2,1)S(1)}, u32[]{:S(2)}, u32[]{:S(2)}) async-start(bf16[8,2,768]{2,1,0:T(2,128)(2,1)} %get-tuple-element.14), calls=%async_computation.1 | async-start | bytes 49152 | tf_op jit(solution)/shard_map/all_to_all | solution.py:275
  18.2 25.1 %all-to-all-start = ((bf16[64,2,896]{2,1,0:T(2,128)(2,1)}), bf16[64,2,896]{2,1,0:T(2,128)(2,1)S(1)}, u32[]{:S(2)}, u32[]{:S(2)}) async-start(bf16[64,2,896]{2,1,0:T(2,128)(2,1)} %get-tuple-element.13), calls=%async_computation | async-start | bytes 458752 | tf_op jit(solution)/shard_map/all_to_all | solution.py:281
  43.4 16.8 %copy-start.3 = (f32[2,128]{1,0:T(2,128)S(1)}, f32[2,128]{1,0:T(2,128)}, u32[]{:S(2)}) copy-start(f32[2,128]{1,0:T(2,128)} %get-tuple-element.16) | copy-start | bytes 3076
  43.7 24.7 %copy-start.1 = (f32[2,768]{1,0:T(2,128)S(1)}, f32[2,768]{1,0:T(2,128)}, u32[]{:S(2)}) copy-start(f32[2,768]{1,0:T(2,128)} %get-tuple-element.15) | copy-start | bytes 18436
  45.3 23.0 %all-to-all-start.2 = ((f32[64,2,768]{2,1,0:T(2,128)}), f32[64,2,768]{2,1,0:T(2,128)S(1)}, u32[]{:S(2)}, u32[]{:S(2)}) async-start(f32[64,2,768]{2,1,0:T(2,128)} %reshape.110), calls=%async_computation.2 | async-start | bytes 786432 | tf_op jit(solution)/shard_map/all_to_all | solution.py:305
  50.2 10.2 %collective-permute-start = (f32[4,896]{1,0:T(4,128)S(1)}, f32[4,896]{1,0:T(4,128)S(1)}, u32[]{:S(2)}, u32[]{:S(2)}) collective-permute-start(f32[4,896]{1,0:T(4,128)S(1)} %get-tuple-element.23), channel_id=1, source_target_pairs={{0,128},{128,256},{256,384},{384,0},{1,129},{129,257},{257,385},{3... | collective-permute-start | bytes 43016 | tf_op jit(solution)/shard_map/ppermute | solution.py:247
  53.4 6.9 %collective-permute-start.2 = (f32[4,896]{1,0:T(4,128)S(1)}, f32[4,896]{1,0:T(4,128)S(1)}, u32[]{:S(2)}, u32[]{:S(2)}) collective-permute-start(f32[4,896]{1,0:T(4,128)S(1)} %get-tuple-element.24), channel_id=1, source_target_pairs={{0,384},{128,0},{256,128},{384,256},{1,385},{129,1},{257,129},{385... | collective-permute-start | bytes 43016 | tf_op jit(solution)/shard_map/ppermute | solution.py:247
  56.7 6.3 %collective-permute-start.1 = (f32[4,896]{1,0:T(4,128)S(1)}, f32[4,896]{1,0:T(4,128)S(1)}, u32[]{:S(2)}, u32[]{:S(2)}) collective-permute-start(f32[4,896]{1,0:T(4,128)S(1)} %get-tuple-element.25), channel_id=1, source_target_pairs={{0,256},{128,384},{256,0},{384,128},{1,257},{129,385},{257,1},{385... | collective-permute-start | bytes 43016 | tf_op jit(solution)/shard_map/ppermute | solution.py:247
  63.0 6.2 %copy-start = (f32[4,896]{1,0:T(4,128)}, f32[4,896]{1,0:T(4,128)S(1)}, u32[]{:S(2)}) copy-start(f32[4,896]{1,0:T(4,128)S(1)} %fusion.11.chip_ref) | copy-start | bytes 43012
  63.0 6.2 %collective-permute-start.3 = (f32[2,896]{1,0:T(2,128)S(1)}, f32[2,896]{1,0:T(2,128)S(1)}, u32[]{:S(2)}, u32[]{:S(2)}) collective-permute-start(f32[2,896]{1,0:T(2,128)S(1)} %slice.96), channel_id=1, source_target_pairs={{0,32},{32,0},{1,33},{33,1},{2,34},{34,2},{3,35},{35,3},{4,36},{36... | collective-permute-start | bytes 21512 | tf_op jit(solution)/shard_map/ppermute | solution.py:243
  69.2 0.6 copy-start.2

commit v8 on v5

--- a/solution.py
+++ b/solution.py
@@ -19,7 +19,7 @@
 ROW_AXES = ("x", "y_lo", "core")
 BLK_AXES = ("z", "y_hi")
 TEXT_AXES = ("x", "core")
-IMAGE_AXES = ("z", "y_hi", "y_lo")
+IMAGE_AXES = ("y_hi", "y_lo", "z")
 
 
 def code_sums(latent):

time: 71.8 us -> 71.6 us (level)
  no operation moved by 1% of the time
where the time goes in v8:
time: 71.6 us; the launch traced here: 71 us
  starting transfers between devices  42.2 us (59%)
  waiting for transfers between devices  14.1 us (20%)
  Pallas kernels  8.81 us (12%)
  between operations  2.2 us (3%)
  local copies, waits for them, and re-layouts  1.99 us (3%)
  other arithmetic  1.15 us (2%)
    all_to_all x1, starting transfers between devices, body(): group_block = lax.all_to_all(image_block, IMAGE_AXES, 0, 0)  12 us
    all_to_all x1, waiting for transfers between devices, body(): group_block = lax.all_to_all(image_block, IMAGE_AXES, 0, 0)  11.4 us
    all_to_all x1, starting transfers between devices, body(): group_text = lax.all_to_all(text_block, TEXT_AXES, 0, 0)  10.1 us
    ppermute x3, starting transfers between devices, along_x(): lax.ppermute(block, 'x', [(i, (i + distance) % count) for i in range(coun...  9.89 us
    pallas_call x1, Pallas kernels, embed_images(): pl.pallas_call(functools.partial(image_kernel, copies), out_shape=(jax.Sh...  5.91 us
    all_to_all x1, starting transfers between devices, body(): image_part = lax.all_to_all(image_part, IMAGE_AXES, 0, 0)  5.22 us
    ppermute x1, starting transfers between devices, swap_cores(): return lax.ppermute(block, 'core', [(0, 1), (1, 0)])  4.99 us
    ppermute x3, waiting for transfers between devices, along_x(): lax.ppermute(block, 'x', [(i, (i + distance) % count) for i in range(coun...  2.72 us
  transfers between devices with their start and end apart: 7, of which 2 were waited for; matrix products, arithmetic and copies ran while one was open for 2% of the time, Pallas kernels for 8%

profile of v8, /device:TPU:1, one launch (start us, length us, event | category | flops | bytes accessed | tf_op | source)
XLA Modules:
  0.0 71.0 jit_solution(9102756895105646280)
XLA Ops:
  0.6 1.4 %text_blocks.1 = (bf16[8,2,768]{2,1,0:T(2,128)(2,1)}, f32[2,768]{1,0:T(2,128)}, f32[2,128]{1,0:T(2,128)}) custom-call(bf16[2,768]{1,0:T(2,128)(2,1)} %text_ref.1), custom_call_target="tpu_custom_call" | custom-call | tf_op jit(solution)/shard_map/text_blocks/pallas_call | solution.py:196
  2.0 10.1 %all-to-all-start.1 = ((bf16[8,2,768]{2,1,0:T(2,128)(2,1)}), bf16[8,2,768]{2,1,0:T(2,128)(2,1)S(1)}, u32[]{:S(2)}, u32[]{:S(2)}) async-start(bf16[8,2,768]{2,1,0:T(2,128)(2,1)} %get-tuple-element.14), calls=%async_computation.1 | async-start | bytes 49152 | tf_op jit(solution)/shard_map/all_to_all | solution.py:275
  12.1 5.9 %embed_images.1 = (bf16[64,2,896]{2,1,0:T(2,128)(2,1)}, f32[2,768]{1,0:T(2,128)}, f32[2,128]{1,0:T(2,128)}) custom-call(f32[28,1024]{1,0:T(8,128)} %latent_hbm.1, bf16[28,1024]{1,0:T(8,128)(2,1)} %post_hbm.1, bf16[1024,768]{1,0:T(8,128)(2,1)} %proj_hbm.1, f32[768]{0:T(1024)} %gain_ref.1, s32[2]{0:T(128)} %label_ref.1), custom_call_target="tpu_custom_call" | custom-call | flops 2200000000 | bytes 1800000 | tf_op jit(solution)/shard_map/embed_images/pallas_call | solution.py:152
  18.1 0.0 all-to-all-done.1
  18.1 12.0 %all-to-all-start = ((bf16[64,2,896]{2,1,0:T(2,128)(2,1)}), bf16[64,2,896]{2,1,0:T(2,128)(2,1)S(1)}, u32[]{:S(2)}, u32[]{:S(2)}) async-start(bf16[64,2,896]{2,1,0:T(2,128)(2,1)} %get-tuple-element.13), calls=%async_computation | async-start | bytes 458752 | tf_op jit(solution)/shard_map/all_to_all | solution.py:281
  31.5 0.1 concatenate.6
  31.6 11.4 %all-to-all-done = bf16[64,2,896]{2,1,0:T(2,128)(2,1)S(1)} async-done(((bf16[64,2,896]{2,1,0:T(2,128)(2,1)}), bf16[64,2,896]{2,1,0:T(2,128)(2,1)S(1)}, u32[]{:S(2)}, u32[]{:S(2)}) %all-to-all-start) | async-done | bytes 229408 | tf_op jit(solution)/shard_map/all_to_all | solution.py:281
  42.9 0.1 reshape.108
  43.0 0.0 copy-start.3
  43.1 0.1 copy.13
  43.2 0.1 convert_reduce_fusion
  43.3 0.0 copy-start.1
  43.3 0.2 fusion.6
  43.5 0.1 fusion.7
  43.7 0.2 fusion.34
  43.9 1.0 %reshape.110 = f32[64,2,768]{2,1,0:T(2,128)} reshape(f32[128,768]{1,0:T(8,128)S(1)} %fusion.34) | data formatting | bytes 786432 | tf_op jit(solution)/shard_map/reshape | solution.py:304
  44.9 5.2 %all-to-all-start.2 = ((f32[64,2,768]{2,1,0:T(2,128)}), f32[64,2,768]{2,1,0:T(2,128)S(1)}, u32[]{:S(2)}, u32[]{:S(2)}) async-start(f32[64,2,768]{2,1,0:T(2,128)} %reshape.110), calls=%async_computation.2 | async-start | bytes 786432 | tf_op jit(solution)/shard_map/all_to_all | solution.py:305
  50.2 3.1 %collective-permute-start = (f32[4,896]{1,0:T(4,128)S(1)}, f32[4,896]{1,0:T(4,128)S(1)}, u32[]{:S(2)}, u32[]{:S(2)}) collective-permute-start(f32[4,896]{1,0:T(4,128)S(1)} %get-tuple-element.23), channel_id=1, source_target_pairs={{0,128},{128,256},{256,384},{384,0},{1,129},{129,257},{257,385},{3... | collective-permute-start | bytes 43016 | tf_op jit(solution)/shard_map/ppermute | solution.py:247
  53.3 3.4 %collective-permute-start.2 = (f32[4,896]{1,0:T(4,128)S(1)}, f32[4,896]{1,0:T(4,128)S(1)}, u32[]{:S(2)}, u32[]{:S(2)}) collective-permute-start(f32[4,896]{1,0:T(4,128)S(1)} %get-tuple-element.24), channel_id=1, source_target_pairs={{0,384},{128,0},{256,128},{384,256},{1,385},{129,1},{257,129},{385... | collective-permute-start | bytes 43016 | tf_op jit(solution)/shard_map/ppermute | solution.py:247
  56.7 3.4 %collective-permute-start.1 = (f32[4,896]{1,0:T(4,128)S(1)}, f32[4,896]{1,0:T(4,128)S(1)}, u32[]{:S(2)}, u32[]{:S(2)}) collective-permute-start(f32[4,896]{1,0:T(4,128)S(1)} %get-tuple-element.25), channel_id=1, source_target_pairs={{0,256},{128,384},{256,0},{384,128},{1,257},{129,385},{257,1},{385... | collective-permute-start | bytes 43016 | tf_op jit(solution)/shard_map/ppermute | solution.py:247
  60.1 0.0 copy-done.3
  60.1 0.1 slice_reduce_fusion
  60.2 0.0 collective-permute-done
  60.2 0.0 collective-permute-done.2
  60.2 2.7 %collective-permute-done.1 = f32[4,896]{1,0:T(4,128)S(1)} collective-permute-done((f32[4,896]{1,0:T(4,128)S(1)}, f32[4,896]{1,0:T(4,128)S(1)}, u32[]{:S(2)}, u32[]{:S(2)}) %collective-permute-start.1) | collective-permute-done | bytes 14368 | tf_op jit(solution)/shard_map/ppermute | solution.py:247
  63.0 0.0 copy-start
  63.0 5.0 %collective-permute-start.3 = (f32[2,896]{1,0:T(2,128)S(1)}, f32[2,896]{1,0:T(2,128)S(1)}, u32[]{:S(2)}, u32[]{:S(2)}) collective-permute-start(f32[2,896]{1,0:T(2,128)S(1)} %slice.96), channel_id=1, source_target_pairs={{0,32},{32,0},{1,33},{33,1},{2,34},{34,2},{3,35},{35,3},{4,36},{36... | collective-permute-start | bytes 21512 | tf_op jit(solution)/shard_map/ppermute | solution.py:243
  68.0 0.0 all-to-all-done.2
  68.0 0.2 reduce_sum.27
  68.1 0.0 copy-done.1
  68.1 0.1 multiply_reduce_fusion
  68.3 0.7 subtract_multiply_fusion
  68.9 0.0 collective-permute-done.3.moved_ref
  68.9 0.0 copy-start.2
  68.9 0.0 copy-done
  68.9 0.6 copy-done.2
  69.5 1.5 %finish_text.1 = (f32[2,768]{1,0:T(2,128)}, f32[3]{0:T(128)}) custom-call(f32[4,896]{1,0:T(4,128)} %copy-done, f32[2,896]{1,0:T(2,128)} %copy-done.2, f32[2,768]{1,0:T(2,128)} %get-tuple-element.19.unit_ref, f32[2,128]{1,0:T(2,128)} %get-tuple-element.20.inv_ref, f32[1]{0:T(128)} %copy.14.scale_ref), custom_call_target="tpu_custom_call" | custom-call | tf_op jit(solution)/shard_map/finish_text/pallas_call | solution.py:230
  (10 shorter events, 0.1 us)
Async XLA Ops:
  2.0 16.0 %all-to-all-start.1 = ((bf16[8,2,768]{2,1,0:T(2,128)(2,1)}), bf16[8,2,768]{2,1,0:T(2,128)(2,1)S(1)}, u32[]{:S(2)}, u32[]{:S(2)}) async-start(bf16[8,2,768]{2,1,0:T(2,128)(2,1)} %get-tuple-element.14), calls=%async_computation.1 | async-start | bytes 49152 | tf_op jit(solution)/shard_map/all_to_all | solution.py:275
  18.1 24.9 %all-to-all-start = ((bf16[64,2,896]{2,1,0:T(2,128)(2,1)}), bf16[64,2,896]{2,1,0:T(2,128)(2,1)S(1)}, u32[]{:S(2)}, u32[]{:S(2)}) async-start(bf16[64,2,896]{2,1,0:T(2,128)(2,1)} %get-tuple-element.13), calls=%async_computation | async-start | bytes 458752 | tf_op jit(solution)/shard_map/all_to_all | solution.py:281
  43.0 17.1 %copy-start.3 = (f32[2,128]{1,0:T(2,128)S(1)}, f32[2,128]{1,0:T(2,128)}, u32[]{:S(2)}) copy-start(f32[2,128]{1,0:T(2,128)} %get-tuple-element.16) | copy-start | bytes 3076
  43.3 24.8 %copy-start.1 = (f32[2,768]{1,0:T(2,128)S(1)}, f32[2,768]{1,0:T(2,128)}, u32[]{:S(2)}) copy-start(f32[2,768]{1,0:T(2,128)} %get-tuple-element.15) | copy-start | bytes 18436
  44.9 23.1 %all-to-all-start.2 = ((f32[64,2,768]{2,1,0:T(2,128)}), f32[64,2,768]{2,1,0:T(2,128)S(1)}, u32[]{:S(2)}, u32[]{:S(2)}) async-start(f32[64,2,768]{2,1,0:T(2,128)} %reshape.110), calls=%async_computation.2 | async-start | bytes 786432 | tf_op jit(solution)/shard_map/all_to_all | solution.py:305
  50.2 10.0 %collective-permute-start = (f32[4,896]{1,0:T(4,128)S(1)}, f32[4,896]{1,0:T(4,128)S(1)}, u32[]{:S(2)}, u32[]{:S(2)}) collective-permute-start(f32[4,896]{1,0:T(4,128)S(1)} %get-tuple-element.23), channel_id=1, source_target_pairs={{0,128},{128,256},{256,384},{384,0},{1,129},{129,257},{257,385},{3... | collective-permute-start | bytes 43016 | tf_op jit(solution)/shard_map/ppermute | solution.py:247
  53.3 6.9 %collective-permute-start.2 = (f32[4,896]{1,0:T(4,128)S(1)}, f32[4,896]{1,0:T(4,128)S(1)}, u32[]{:S(2)}, u32[]{:S(2)}) collective-permute-start(f32[4,896]{1,0:T(4,128)S(1)} %get-tuple-element.24), channel_id=1, source_target_pairs={{0,384},{128,0},{256,128},{384,256},{1,385},{129,1},{257,129},{385... | collective-permute-start | bytes 43016 | tf_op jit(solution)/shard_map/ppermute | solution.py:247
  56.7 6.3 %collective-permute-start.1 = (f32[4,896]{1,0:T(4,128)S(1)}, f32[4,896]{1,0:T(4,128)S(1)}, u32[]{:S(2)}, u32[]{:S(2)}) collective-permute-start(f32[4,896]{1,0:T(4,128)S(1)} %get-tuple-element.25), channel_id=1, source_target_pairs={{0,256},{128,384},{256,0},{384,128},{1,257},{129,385},{257,1},{385... | collective-permute-start | bytes 43016 | tf_op jit(solution)/shard_map/ppermute | solution.py:247
  63.0 6.0 %copy-start = (f32[4,896]{1,0:T(4,128)}, f32[4,896]{1,0:T(4,128)S(1)}, u32[]{:S(2)}) copy-start(f32[4,896]{1,0:T(4,128)S(1)} %fusion.11.chip_ref) | copy-start | bytes 43012
  63.0 6.0 %collective-permute-start.3 = (f32[2,896]{1,0:T(2,128)S(1)}, f32[2,896]{1,0:T(2,128)S(1)}, u32[]{:S(2)}, u32[]{:S(2)}) collective-permute-start(f32[2,896]{1,0:T(2,128)S(1)} %slice.96), channel_id=1, source_target_pairs={{0,32},{32,0},{1,33},{33,1},{2,34},{34,2},{3,35},{35,3},{4,36},{36... | collective-permute-start | bytes 21512 | tf_op jit(solution)/shard_map/ppermute | solution.py:243
  68.9 0.6 copy-start.2
